TPU v7x, 256 devices: a whole 4x4x8 slice. The times are simulated.
256 devices in a mesh: dp: 64 (over z, y, core), tensor: 4 (over x).
Axes of the slice: x: 4, y: 4, z: 8, core: 2. Of those that a mesh axis runs over, the one named last changes fastest.
Arguments:
- queries: bfloat16 [32768, 8192], P(('dp', 'tensor')), may hold values from -20 to 20
- resp_keys: bfloat16 [32768, 1024], P(('dp', 'tensor')), may hold values from -6 to 6
- resp_values: bfloat16 [32768, 1024], P(('dp', 'tensor')), may hold values from -6 to 6
- grad_output: bfloat16 [32768, 8192], P(('dp', 'tensor')), may hold values from -6 to 6
- prompt_keys: bfloat16 [512, 1024], P('dp', 'tensor'), may hold values from -6 to 6
- prompt_values: bfloat16 [512, 1024], P('dp', 'tensor'), may hold values from -6 to 6
- segment_ids: int32 [64, 512], P('dp'), may hold values from 0 to 1, never falling along the last dimension, each value on 1 to 384 neighbouring positions
- response_group: int32 [64, 2], P('dp'), may hold values from 0 to 3
Outputs:
- grad_queries: bfloat16 [32768, 8192], P(('dp', 'tensor'))
- grad_resp_keys: bfloat16 [32768, 1024], P(('dp', 'tensor'))
- grad_resp_values: bfloat16 [32768, 1024], P(('dp', 'tensor'))
- grad_prompt_keys: float32 [512, 1024], P('dp', 'tensor')
- grad_prompt_values: float32 [512, 1024], P('dp', 'tensor')
Inputs may be any that keep to these rules, and one draw needn't show every extreme that they name: `segment_ids`: each row holds the 2 responses of one dp index in order, each of 128 to 384 neighbouring positions, their lengths summing to 512.
All inputs are finite; a program needn't handle non-finite values.
Results may differ from a plain program's by a relative error of at most 0.015.
Values may be sent and summed in bfloat16 or wider, within the bound.
No kernel may reach another device: no remote copies, remote signals or barrier semaphores. Data moves between devices by JAX's collectives and lax.ppermute only.
A program may use at most 128 MiB of HBM per device.

v0:
```python
import jax
import jax.numpy as jnp
from jax import lax
from jax.sharding import PartitionSpec as P

HD = 128
PLEN = 128
RESP_DEV = 2


neg_large = -1e30


def head_terms(query_block, grad_block, all_keys, all_values, allowed):
    factor = all_keys.shape[-1] ** (-0.5)
    scores = (
        jnp.einsum("tre,ke->trk", query_block, all_keys, preferred_element_type=jnp.float32)
        * factor
    )
    scores = jnp.where(allowed[:, None, :], scores, neg_large)
    row_max = jnp.max(scores, axis=2, keepdims=True)
    log_total = row_max + jnp.log(jnp.sum(jnp.exp(scores - row_max), axis=2, keepdims=True))
    weights = jnp.exp(scores - log_total)
    probs = weights.astype(jnp.bfloat16)
    attended = jnp.einsum("trk,ke->tre", probs, all_values, preferred_element_type=jnp.float32)
    deltas = jnp.sum(grad_block.astype(jnp.float32) * attended, axis=2, keepdims=True)
    grad_probs = jnp.einsum(
        "tre,ke->trk", grad_block, all_values, preferred_element_type=jnp.float32
    )
    grad_scores = (weights * (grad_probs - deltas)).astype(jnp.bfloat16)
    grad_query = (
        jnp.einsum("trk,ke->tre", grad_scores, all_keys, preferred_element_type=jnp.float32)
        * factor
    )
    grad_keys = (
        jnp.einsum("trk,tre->ke", grad_scores, query_block, preferred_element_type=jnp.float32)
        * factor
    )
    grad_values = jnp.einsum("trk,tre->ke", probs, grad_block, preferred_element_type=jnp.float32)
    return (grad_query, grad_keys, grad_values)


def build_mask(query_pos, query_segment, key_segment):
    block_owner = jnp.arange(RESP_DEV * PLEN, dtype=jnp.int32) // PLEN
    prompt_ok = block_owner[None, :] == query_segment[:, None]
    key_pos = jnp.arange(key_segment.shape[0], dtype=jnp.int32)
    self_ok = (query_segment[:, None] == key_segment[None, :]) & (
        key_pos[None, :] <= query_pos[:, None]
    )
    return jnp.concatenate([prompt_ok, self_ok], axis=1)


def pick_prompts(gathered_k, gathered_v, groups_here):
    picked_k, picked_v = ([], [])
    for resp in range(RESP_DEV):
        start = groups_here[resp] * PLEN
        picked_k.append(lax.dynamic_slice_in_dim(gathered_k, start, PLEN, 0))
        picked_v.append(lax.dynamic_slice_in_dim(gathered_v, start, PLEN, 0))
    return (jnp.concatenate(picked_k, axis=0), jnp.concatenate(picked_v, axis=0))


def place_prompts(block_grad, groups_here, prompt_total):
    placed = jnp.zeros((prompt_total, block_grad.shape[1]), jnp.float32)
    for resp in range(RESP_DEV):
        start = groups_here[resp] * PLEN
        current = lax.dynamic_slice_in_dim(placed, start, PLEN, 0)
        placed = lax.dynamic_update_slice_in_dim(
            placed, current + block_grad[resp * PLEN : (resp + 1) * PLEN], start, 0
        )
    return placed


def all_heads(query_cols, grad_cols, self_keys, self_values, prompt_k, prompt_v, allowed):
    kv_count = self_keys.shape[1] // HD
    group_cols = query_cols.shape[1] // kv_count
    per_group = group_cols // HD
    row_count = query_cols.shape[0]
    prompt_count = prompt_k.shape[0]
    query_parts, key_parts, value_parts, prompt_key_parts, prompt_value_parts = ([], [], [], [], [])
    for kv_head in range(kv_count):
        query_block = query_cols[:, kv_head * group_cols : (kv_head + 1) * group_cols].reshape(
            row_count, per_group, HD
        )
        grad_block = grad_cols[:, kv_head * group_cols : (kv_head + 1) * group_cols].reshape(
            row_count, per_group, HD
        )
        all_keys = jnp.concatenate(
            [
                prompt_k[:, kv_head * HD : (kv_head + 1) * HD],
                self_keys[:, kv_head * HD : (kv_head + 1) * HD],
            ],
            axis=0,
        )
        all_values = jnp.concatenate(
            [
                prompt_v[:, kv_head * HD : (kv_head + 1) * HD],
                self_values[:, kv_head * HD : (kv_head + 1) * HD],
            ],
            axis=0,
        )
        grad_query, grad_keys, grad_values = head_terms(
            query_block, grad_block, all_keys, all_values, allowed
        )
        query_parts.append(grad_query.reshape(row_count, group_cols))
        key_parts.append(grad_keys[prompt_count:])
        value_parts.append(grad_values[prompt_count:])
        prompt_key_parts.append(grad_keys[:prompt_count])
        prompt_value_parts.append(grad_values[:prompt_count])
    return (
        jnp.concatenate(query_parts, axis=1),
        jnp.concatenate(key_parts, axis=1),
        jnp.concatenate(value_parts, axis=1),
        jnp.concatenate(prompt_key_parts, axis=1),
        jnp.concatenate(prompt_value_parts, axis=1),
    )


def on_device(
    queries,
    resp_keys,
    resp_values,
    grad_output,
    prompt_keys,
    prompt_values,
    segment_ids,
    response_group,
):
    token_segment = segment_ids[0]
    groups_here = response_group[0]
    prompt_total = prompt_keys.shape[0] * lax.axis_size("dp")
    full_keys, full_values = (
        lax.all_gather(resp_keys, "tensor", axis=0, tiled=True),
        lax.all_gather(resp_values, "tensor", axis=0, tiled=True),
    )
    wide_k, wide_v = (
        lax.all_gather(prompt_keys, "tensor", axis=1, tiled=True),
        lax.all_gather(prompt_values, "tensor", axis=1, tiled=True),
    )
    gathered_k, gathered_v = (
        lax.all_gather(wide_k, "dp", axis=0, tiled=True),
        lax.all_gather(wide_v, "dp", axis=0, tiled=True),
    )
    chosen_k, chosen_v = pick_prompts(gathered_k, gathered_v, groups_here)
    row_count = queries.shape[0]
    first_row = lax.axis_index("tensor") * row_count
    query_pos = first_row + jnp.arange(row_count, dtype=jnp.int32)
    query_segment = lax.dynamic_slice_in_dim(token_segment, first_row, row_count)
    allowed = build_mask(query_pos, query_segment, token_segment)
    grad_query, grad_keys, grad_values, block_grad_k, block_grad_v = all_heads(
        queries, grad_output, full_keys, full_values, chosen_k, chosen_v, allowed
    )
    prompt_grad_k = place_prompts(block_grad_k, groups_here, prompt_total)
    prompt_grad_v = place_prompts(block_grad_v, groups_here, prompt_total)
    out_query = grad_query.astype(jnp.bfloat16)
    summed_k, summed_v = (
        lax.psum_scatter(grad_keys, "tensor", scatter_dimension=0, tiled=True),
        lax.psum_scatter(grad_values, "tensor", scatter_dimension=0, tiled=True),
    )
    out_keys = summed_k.astype(jnp.bfloat16)
    out_values = summed_v.astype(jnp.bfloat16)
    rows_k, rows_v = (
        lax.psum_scatter(prompt_grad_k, "dp", scatter_dimension=0, tiled=True),
        lax.psum_scatter(prompt_grad_v, "dp", scatter_dimension=0, tiled=True),
    )
    owned_k, owned_v = (
        lax.psum_scatter(rows_k, "tensor", scatter_dimension=1, tiled=True),
        lax.psum_scatter(rows_v, "tensor", scatter_dimension=1, tiled=True),
    )
    return (out_query, out_keys, out_values, owned_k, owned_v)


def solution(mesh):
    placed = (
        P(("dp", "tensor"), None),
        P(("dp", "tensor"), None),
        P(("dp", "tensor"), None),
        P(("dp", "tensor"), None),
        P("dp", "tensor"),
        P("dp", "tensor"),
        P("dp", None),
        P("dp", None),
    )
    return jax.shard_map(
        on_device,
        mesh=mesh,
        in_specs=placed,
        out_specs=(
            P(("dp", "tensor"), None),
            P(("dp", "tensor"), None),
            P(("dp", "tensor"), None),
            P("dp", "tensor"),
            P("dp", "tensor"),
        ),
        check_vma=False,
    )
```

profile of v0, /device:TPU:1, one launch (start us, length us, event | category | flops | bytes accessed | tf_op | source)
XLA Modules:
  0.0 596.6 jit_solution(12263760838742703403)
XLA Ops:
  8.7 11.7 %all_gather.21 = bf16[8,1024]{1,0:T(8,128)(2,1)} all-gather(bf16[8,256]{1,0:T(8,128)(2,1)} %param.13), channel_id=1, replica_groups=mesh['dp'=64,'tensor'=4] {'tensor'}, dimensions={1}, use_global_device_ids=true | all-gather | bytes 20480 | tf_op jit(solution)/shard_map/all_gather | solution.py:137
  20.5 10.1 %all_gather.18 = bf16[8,1024]{1,0:T(8,128)(2,1)} all-gather(bf16[8,256]{1,0:T(8,128)(2,1)} %param.12), channel_id=1, replica_groups=mesh['dp'=64,'tensor'=4] {'tensor'}, dimensions={1}, use_global_device_ids=true | all-gather | bytes 20480 | tf_op jit(solution)/shard_map/all_gather | solution.py:136
  30.7 1.8 fusion.122
  35.8 2.5 fusion.121
  38.3 1.8 copy.380
  40.1 1.8 copy.378
  41.9 1.8 copy.376
  48.3 2.0 fusion.124
  50.3 17.3 %all-gather.11.cloned.1.call-done = bf16[512,1024]{1,0:T(8,128)(2,1)} async-done(((bf16[128,1024]{1,0:T(8,128)(2,1)}), bf16[512,1024]{1,0:T(8,128)(2,1)}) %all-gather.11.cloned.1.call-update) | async-done | bytes 1048592 | tf_op jit(solution)/shard_map/all_gather | solution.py:133
  67.6 2.3 fusion.123
  69.9 79.2 %all-gather.9.cloned.1.call-done = bf16[512,1024]{1,0:T(8,128)(2,1)} async-done(((bf16[8,1024]{1,0:T(8,128)(2,1)}), bf16[512,1024]{1,0:T(8,128)(2,1)}) %all-gather.9.cloned.1.call-update) | async-done | bytes 1048592 | tf_op jit(solution)/shard_map/all_gather | solution.py:141
  151.7 74.1 %all-gather.5.cloned.1.call-done = bf16[512,1024]{1,0:T(8,128)(2,1)} async-done(((bf16[8,1024]{1,0:T(8,128)(2,1)}), bf16[512,1024]{1,0:T(8,128)(2,1)}) %all-gather.5.cloned.1.call-update) | async-done | bytes 1048592 | tf_op jit(solution)/shard_map/all_gather | solution.py:140
  231.7 5.0 exponential_reduce_fusion
  238.7 4.5 exponential_reduce_fusion.1
  281.1 184.0 %all-reduce.5.cloned.1.call-done = (f32[512,1024]{0,1:T(8,128)}, f32[512,1024]{0,1:T(8,128)}) async-done(((f32[512,1024]{0,1:T(8,128)}, f32[512,1024]{0,1:T(8,128)}), (f32[512,1024]{0,1:T(8,128)}, f32[512,1024]{0,1:T(8,128)})) %all-reduce.5.cloned.1.call-update) | async-done | bytes 4194320
  465.1 2.0 constant_dynamic-slice_fusion.5
  467.3 2.1 constant_dynamic-slice_fusion.6
  476.6 2.7 fusion.28
  480.5 2.5 fusion.27
  484.8 2.0 fusion.26
  486.9 1.9 copy.255
  488.8 2.0 fusion.25
  490.8 1.9 copy.254
  492.7 2.0 fusion.30
  494.8 1.9 copy.259
  496.7 2.0 fusion.29
  498.7 1.9 copy.258
  500.6 2.0 fusion.24
  502.6 1.9 copy.253
  504.5 2.1 fusion.31
  518.3 34.9 %reduce-scatter.9.cloned.1.call-done = f32[128,1024]{0,1:T(8,128)} async-done(((f32[512,1024]{0,1:T(8,128)}), f32[128,1024]{0,1:T(8,128)}) %reduce-scatter.9.cloned.1.call-update) | async-done | bytes 524304 | tf_op jit(solution)/shard_map/reduce_scatter | solution.py:157
  555.1 32.6 %reduce-scatter.7.cloned.1.call-done = f32[128,1024]{0,1:T(8,128)} async-done(((f32[512,1024]{0,1:T(8,128)}), f32[128,1024]{0,1:T(8,128)}) %reduce-scatter.7.cloned.1.call-update) | async-done | bytes 524304 | tf_op jit(solution)/shard_map/reduce_scatter | solution.py:156
  (309 shorter events, 80.2 us)
Async XLA Ops:
  7.2 25.3 %copy-start.79 = (s32[1,2]{1,0:T(1,128)S(1)}, s32[1,2]{1,0:T(1,128)}, u32[]{:S(2)}) copy-start(s32[1,2]{1,0:T(1,128)} %param.15) | copy-start | bytes 28
  7.2 41.1 %all-gather.7.cloned.1.call-start = ((), (), s32[]{:S(2)}) async-start(), calls=%async_computation.5 | async-start | bytes 1310720 | tf_op jit(solution)/shard_map/all_gather | solution.py:132
  7.9 59.7 %all-gather.11.cloned.1.call-start = ((), (), s32[]{:S(2)}) async-start(), calls=%async_computation.7 | async-start | bytes 1310720 | tf_op jit(solution)/shard_map/all_gather | solution.py:133
  8.7 140.4 %all-gather.9.cloned.1.call-start = ((), (), s32[]{:S(2)}) async-start(), calls=%async_computation.6 | async-start | bytes 1064960 | tf_op jit(solution)/shard_map/all_gather | solution.py:141
  20.5 205.3 %all-gather.5.cloned.1.call-start = ((), (), s32[]{:S(2)}) async-start(), calls=%async_computation.4 | async-start | bytes 1064960 | tf_op jit(solution)/shard_map/all_gather | solution.py:140
  30.7 434.5 %all-reduce.5.cloned.1.call-start = ((), (), s32[]{:S(2)}) async-start(), calls=%async_computation.12 | async-start | bytes 8388608
  38.3 9.6 %copy-start.78 = (s32[1,512]{1,0:T(1,128)S(1)}, s32[1,512]{1,0:T(1,128)}, u32[]{:S(2)}) copy-start(s32[1,512]{1,0:T(1,128)} %param.14) | copy-start | bytes 6148
  50.3 177.3 %copy-start.33 = (bf16[512,128]{1,0:T(8,128)(2,1)}, bf16[512,128]{1,0:T(8,128)(2,1)S(1)}, u32[]{:S(2)}) copy-start(bf16[512,128]{1,0:T(8,128)(2,1)S(1)} %get-tuple-element.67) | copy-start | bytes 393220
  50.3 177.9 %copy-start.34 = (bf16[512,128]{1,0:T(8,128)(2,1)}, bf16[512,128]{1,0:T(8,128)(2,1)S(1)}, u32[]{:S(2)}) copy-start(bf16[512,128]{1,0:T(8,128)(2,1)S(1)} %get-tuple-element.66) | copy-start | bytes 393220
  50.3 178.5 %copy-start.35 = (bf16[512,128]{1,0:T(8,128)(2,1)}, bf16[512,128]{1,0:T(8,128)(2,1)S(1)}, u32[]{:S(2)}) copy-start(bf16[512,128]{1,0:T(8,128)(2,1)S(1)} %get-tuple-element.65) | copy-start | bytes 393220
  50.3 179.1 %copy-start.31 = (bf16[512,128]{1,0:T(8,128)(2,1)}, bf16[512,128]{1,0:T(8,128)(2,1)S(1)}, u32[]{:S(2)}) copy-start(bf16[512,128]{1,0:T(8,128)(2,1)S(1)} %get-tuple-element.64) | copy-start | bytes 393220
  50.3 179.6 %copy-start.32 = (bf16[512,128]{1,0:T(8,128)(2,1)}, bf16[512,128]{1,0:T(8,128)(2,1)S(1)}, u32[]{:S(2)}) copy-start(bf16[512,128]{1,0:T(8,128)(2,1)S(1)} %get-tuple-element.62) | copy-start | bytes 393220
  237.8 33.4 %copy-start.37 = (f32[768,128]{0,1:T(8,128)}, f32[768,128]{0,1:T(8,128)S(1)}, u32[]{:S(2)}) copy-start(f32[768,128]{0,1:T(8,128)S(1)} %convolution_bitcast_fusion) | copy-start | bytes 1179652
  244.2 26.9 %copy-start.38 = (f32[768,128]{0,1:T(8,128)}, f32[768,128]{0,1:T(8,128)S(1)}, u32[]{:S(2)}) copy-start(f32[768,128]{0,1:T(8,128)S(1)} %convolution_bitcast_fusion.3) | copy-start | bytes 1179652
  247.8 23.4 %copy-start.39 = (f32[768,128]{0,1:T(8,128)}, f32[768,128]{0,1:T(8,128)S(1)}, u32[]{:S(2)}) copy-start(f32[768,128]{0,1:T(8,128)S(1)} %convolution_bitcast_fusion.4) | copy-start | bytes 1179652
  251.4 19.7 %copy-start.40 = (f32[768,128]{0,1:T(8,128)}, f32[768,128]{0,1:T(8,128)S(1)}, u32[]{:S(2)}) copy-start(f32[768,128]{0,1:T(8,128)S(1)} %convolution_bitcast_fusion.5) | copy-start | bytes 1179652
  254.9 16.1 %copy-start.41 = (f32[768,128]{0,1:T(8,128)}, f32[768,128]{0,1:T(8,128)S(1)}, u32[]{:S(2)}) copy-start(f32[768,128]{0,1:T(8,128)S(1)} %convolution_bitcast_fusion.6) | copy-start | bytes 1179652
  257.6 12.7 %copy-start.18 = (f32[768,128]{0,1:T(8,128)}, f32[768,128]{0,1:T(8,128)S(1)}, u32[]{:S(2)}) copy-start(f32[768,128]{0,1:T(8,128)S(1)} %fusion.38) | copy-start | bytes 1179652
  258.7 12.5 %copy-start.42 = (f32[768,128]{0,1:T(8,128)}, f32[768,128]{0,1:T(8,128)S(1)}, u32[]{:S(2)}) copy-start(f32[768,128]{0,1:T(8,128)S(1)} %convolution_bitcast_fusion.1) | copy-start | bytes 1179652
  261.4 9.0 %copy-start.19 = (f32[768,128]{0,1:T(8,128)}, f32[768,128]{0,1:T(8,128)S(1)}, u32[]{:S(2)}) copy-start(f32[768,128]{0,1:T(8,128)S(1)} %fusion.33) | copy-start | bytes 1179652
  262.3 8.9 %copy-start.44 = (f32[768,128]{0,1:T(8,128)}, f32[768,128]{0,1:T(8,128)S(1)}, u32[]{:S(2)}) copy-start(f32[768,128]{0,1:T(8,128)S(1)} %convolution_bitcast_fusion.2) | copy-start | bytes 1179652
  273.9 240.5 %reduce-scatter.13.cloned.1.call-start = ((), (), s32[]{:S(2)}) async-start(), calls=%async_computation.11 | async-start | bytes 655360 | tf_op jit(solution)/shard_map/reduce_scatter | solution.py:167
  467.2 49.5 %reduce-scatter.11.cloned.1.call-start = ((), (), s32[]{:S(2)}) async-start(), calls=%async_computation.10 | async-start | bytes 655360 | tf_op jit(solution)/shard_map/reduce_scatter | solution.py:166
  469.3 83.9 %reduce-scatter.9.cloned.1.call-start = ((), (), s32[]{:S(2)}) async-start(), calls=%async_computation.9 | async-start | bytes 2621440 | tf_op jit(solution)/shard_map/reduce_scatter | solution.py:157
  471.8 116.0 %reduce-scatter.7.cloned.1.call-start = ((), (), s32[]{:S(2)}) async-start(), calls=%async_computation.8 | async-start | bytes 2621440 | tf_op jit(solution)/shard_map/reduce_scatter | solution.py:156
  476.6 8.2 %copy-start.7 = (bf16[128,8,768]{0,2,1:T(8,128)(2,1)S(1)}, bf16[128,8,768]{0,2,1:T(8,128)(2,1)}, u32[]{:S(2)}) copy-start(bf16[128,8,768]{0,2,1:T(8,128)(2,1)} %copy-done.6) | copy-start | bytes 4718596
  479.3 9.5 %copy-start.9 = (bf16[128,8,768]{0,2,1:T(8,128)(2,1)S(1)}, bf16[128,8,768]{0,2,1:T(8,128)(2,1)}, u32[]{:S(2)}) copy-start(bf16[128,8,768]{0,2,1:T(8,128)(2,1)} %copy-done.8) | copy-start | bytes 4718596
  502.6 6.7 %copy-start.28 = (bf16[128,1024]{1,0:T(8,128)(2,1)S(1)}, bf16[128,1024]{1,0:T(8,128)(2,1)}, u32[]{:S(2)}) copy-start(bf16[128,1024]{1,0:T(8,128)(2,1)} %copy.254) | copy-start | bytes 786436
  502.6 7.5 %copy-start.26 = (bf16[128,1024]{1,0:T(8,128)(2,1)S(1)}, bf16[128,1024]{1,0:T(8,128)(2,1)}, u32[]{:S(2)}) copy-start(bf16[128,1024]{1,0:T(8,128)(2,1)} %copy.255) | copy-start | bytes 786436
  502.6 8.2 %copy-start.25 = (bf16[128,1024]{1,0:T(8,128)(2,1)S(1)}, bf16[128,1024]{1,0:T(8,128)(2,1)}, u32[]{:S(2)}) copy-start(bf16[128,1024]{1,0:T(8,128)(2,1)} %copy.256) | copy-start | bytes 786436
  502.6 9.6 %copy-start.29 = (bf16[128,1024]{1,0:T(8,128)(2,1)S(1)}, bf16[128,1024]{1,0:T(8,128)(2,1)}, u32[]{:S(2)}) copy-start(bf16[128,1024]{1,0:T(8,128)(2,1)} %copy.258) | copy-start | bytes 786436
  502.6 10.3 %copy-start.27 = (bf16[128,1024]{1,0:T(8,128)(2,1)S(1)}, bf16[128,1024]{1,0:T(8,128)(2,1)}, u32[]{:S(2)}) copy-start(bf16[128,1024]{1,0:T(8,128)(2,1)} %copy.259) | copy-start | bytes 786436
  (58 other events, 142.1 us)
Sparse Core Ops, SparseCore 0:
  9.8 29.3 all-gather.6
  41.1 26.5 all-gather.10
  70.4 78.6 all-gather.8
  151.7 74.0 all-gather.4
  274.0 191.0 all-reduce.4
  467.7 22.5 reduce-scatter.12
  493.0 23.6 reduce-scatter.10
  519.5 33.6 reduce-scatter.8
  555.8 31.9 reduce-scatter.6
where the time goes:
time: 607 us; the launch traced here: 597 us
  waiting for transfers between devices  424 us (70%)
  local copies, waits for them, and re-layouts  68.1 us (11%)
  matrix products  54.7 us (9%)
  blocking collectives  21.9 us (4%)
  between operations  18 us (3%)
  other arithmetic  8.9 us (1%)
    unnamed x10, waiting for transfers between devices  186 us
    all_gather x1, waiting for transfers between devices, on_device(): lax.all_gather(wide_v, 'dp', axis=0, tiled=True)  79.2 us
    all_gather x1, waiting for transfers between devices, on_device(): lax.all_gather(wide_k, 'dp', axis=0, tiled=True)  74.1 us
    unnamed x220, local copies, waits for them, and re-layouts  40.9 us
    reduce_scatter x1, waiting for transfers between devices, on_device(): lax.psum_scatter(grad_values, 'tensor', scatter_dimension=0, tiled=True)  34.9 us
    reduce_scatter x1, waiting for transfers between devices, on_device(): lax.psum_scatter(grad_keys, 'tensor', scatter_dimension=0, tiled=True)  32.6 us
    dot_general x8, matrix products, head_terms(): jnp.einsum('trk,ke->tre', grad_scores, all_keys, preferred_element_type=j...  17.3 us
    all_gather x1, waiting for transfers between devices, on_device(): lax.all_gather(resp_values, 'tensor', axis=0, tiled=True)  17.3 us
  transfers between devices with their start and end apart: 9, of which 7 were waited for; matrix products, arithmetic and copies ran while one was open for 13% of the time, Pallas kernels for 0%

commit v1 on v0

v1 whole, which is shorter than its diff:
```python
import functools
import math

import jax
import jax.numpy as jnp
from jax import lax
from jax.experimental import pallas as pl
from jax.experimental.pallas import tpu as pltpu
from jax.sharding import Mesh, PartitionSpec as P

HD = 128
BLK = 128
HEAD_COLS = 1024
KV_HEADS = 8
N_X = 4
FACTOR = HD**-0.5
LOG2_SCALE = FACTOR * math.log2(math.e)
NEG = -1e30
bf16, f32 = jnp.bfloat16, jnp.float32


def dot_nt(a, b):
    return lax.dot_general(a, b, (((1,), (1,)), ((), ())), preferred_element_type=f32)


def dot_nn(a, b):
    return lax.dot_general(a, b, (((1,), (0,)), ((), ())), preferred_element_type=f32)


def attention_kernel(
    sc_ref, q_ref, do_ref, ko_ref, vo_ref, near_ref, far_ref, pr_ref, *refs
):
    dq_ref, own_ref, dnear_ref, dfar_ref, dpr_ref = refs[-5:]
    place, border = sc_ref[1], sc_ref[2]

    def wide(x):
        return jnp.concatenate([x, x], axis=1)

    u = lax.broadcasted_iota(jnp.int32, (3 * BLK, BLK), 0) + (place - 2) * BLK
    t = lax.broadcasted_iota(jnp.int32, (3 * BLK, BLK), 1) + place * BLK
    ok = (u >= 0) & (u <= t) & ((u >= border) == (t >= border))
    bias = wide(jnp.where(ok, 0.0, NEG).astype(f32))
    row_t = lax.broadcasted_iota(jnp.int32, (2 * BLK, HD), 0) % BLK + place * BLK
    first = jnp.where(row_t < border, 1.0, 0.0).astype(bf16)
    second = jnp.where(row_t < border, 0.0, 1.0).astype(bf16)
    lane_t = lax.broadcasted_iota(jnp.int32, (HD, 2 * BLK), 1) % BLK + place * BLK
    lane_first = lane_t < border

    k_r = jnp.concatenate([far_ref[0], near_ref[0], ko_ref[...]], axis=0)
    v_r = jnp.concatenate([far_ref[1], near_ref[1], vo_ref[...]], axis=0)
    k_p = jnp.concatenate([pr_ref[0, 0], pr_ref[1, 0]], axis=1)
    v_p = jnp.concatenate([pr_ref[0, 1], pr_ref[1, 1]], axis=1)
    k_r_t = k_r.T
    k_p_t = k_p.T

    dk_r = dv_r = dk_p = dv_p = None
    for pair in range(4):
        cols = [slice((2 * pair + j) * HD, (2 * pair + j + 1) * HD) for j in range(2)]
        q = jnp.concatenate([q_ref[:, c] for c in cols], axis=0)
        do = jnp.concatenate([do_ref[:, c] for c in cols], axis=0)
        q_two = jnp.concatenate([q * first, q * second], axis=1)
        do_two = jnp.concatenate([do * first, do * second], axis=1)
        s_p = dot_nt(k_p, q_two)
        s_r = dot_nt(k_r, q) + bias
        top = jnp.maximum(
            jnp.max(s_p, axis=0, keepdims=True), jnp.max(s_r, axis=0, keepdims=True)
        )
        e_p = jnp.exp2((s_p - top) * LOG2_SCALE)
        e_r = jnp.exp2((s_r - top) * LOG2_SCALE)
        total = jnp.sum(e_p, axis=0, keepdims=True) + jnp.sum(e_r, axis=0, keepdims=True)
        inv = 1.0 / total
        w_p = e_p * inv
        w_r = e_r * inv
        p_p = w_p.astype(bf16)
        p_r = w_r.astype(bf16)
        g_p = dot_nt(v_p, do_two)
        g_r = dot_nt(v_r, do)
        delta = jnp.sum(p_p.astype(f32) * g_p, axis=0, keepdims=True) + jnp.sum(
            p_r.astype(f32) * g_r, axis=0, keepdims=True
        )
        ds_p = (w_p * (g_p - delta)).astype(bf16)
        ds_r = (w_r * (g_r - delta)).astype(bf16)
        dq_two = dot_nn(k_p_t, ds_p)
        dq_t = dot_nn(k_r_t, ds_r) + jnp.where(lane_first, dq_two[:HD], dq_two[HD:])
        dq = (dq_t * FACTOR).T.astype(bf16)
        for j in range(2):
            dq_ref[:, cols[j]] = dq[j * BLK : (j + 1) * BLK]
        parts = (dot_nn(ds_r, q), dot_nn(p_r, do), dot_nn(ds_p, q_two), dot_nn(p_p, do_two))
        if pair == 0:
            dk_r, dv_r, dk_p, dv_p = parts
        else:
            dk_r, dv_r, dk_p, dv_p = (
                dk_r + parts[0],
                dv_r + parts[1],
                dk_p + parts[2],
                dv_p + parts[3],
            )
    dk_r = dk_r * FACTOR
    dk_p = dk_p * FACTOR
    for j, grad in enumerate((dk_r, dv_r)):
        dfar_ref[j] = grad[:BLK].astype(bf16)
        dnear_ref[j] = grad[BLK : 2 * BLK].astype(bf16)
        own_ref[j] = grad[2 * BLK :]
    for j, grad in enumerate((dk_p, dv_p)):
        dpr_ref[0, j] = grad[:, :HD].astype(bf16)
        dpr_ref[1, j] = grad[:, HD:].astype(bf16)


def attend(scalars, q, do, rk, rv, near, far, prompts, carried):
    def at_head(i, sc):
        return (0, sc[0] + i)

    def pair_at_head(i, sc):
        return (0, 0, sc[0] + i)

    wide_spec = pl.BlockSpec((BLK, HEAD_COLS), at_head)
    one_spec = pl.BlockSpec((BLK, HD), at_head)
    pair_spec = pl.BlockSpec((2, BLK, HD), pair_at_head)
    prompt_spec = pl.BlockSpec((2, 2, BLK, HD), lambda i, sc: (0, 0, 0, i))
    out_shape = (
        jax.ShapeDtypeStruct((BLK, KV_HEADS * HEAD_COLS), bf16),
        jax.ShapeDtypeStruct((2, BLK, KV_HEADS * HD), f32),
        jax.ShapeDtypeStruct((2, BLK, KV_HEADS * HD), bf16),
        jax.ShapeDtypeStruct((2, BLK, KV_HEADS * HD), bf16),
        jax.ShapeDtypeStruct((2, 2, BLK, 2 * HD), bf16),
    )
    in_specs = [
        wide_spec,
        wide_spec,
        one_spec,
        one_spec,
        pair_spec,
        pair_spec,
        prompt_spec,
    ]
    aliases = {}
    operands = [q, do, rk, rv, near, far, prompts]
    if carried is not None:
        for k, array in enumerate(carried):
            aliases[1 + len(operands)] = k
            operands.append(array)
            in_specs.append(pl.BlockSpec(memory_space=pl.ANY))
    return pl.pallas_call(
        attention_kernel,
        out_shape=out_shape,
        grid_spec=pltpu.PrefetchScalarGridSpec(
            num_scalar_prefetch=1,
            grid=(2,),
            in_specs=in_specs,
            out_specs=(wide_spec, pair_spec, pair_spec, pair_spec, prompt_spec),
        ),
        input_output_aliases=aliases,
        compiler_params=pltpu.CompilerParams(vmem_limit_bytes=32 * 1024 * 1024),
        cost_estimate=pl.CostEstimate(
            flops=5 * 2 * 1024 * 512 * 128 * 2 * 2, bytes_accessed=4 << 20, transcendentals=1 << 20
        ),
    )(scalars, *operands)


def shift(a, axis, size, by):
    return lax.ppermute(a, axis, [(i, (i + by) % size) for i in range(size)])


def on_device(q, rk, rv, do, pk, pv, segment_ids, response_group):
    x = lax.axis_index("x")
    core = lax.axis_index("core")
    groups = response_group[0]
    border = jnp.sum((segment_ids[0] == 0).astype(jnp.int32))

    kv = jnp.stack([rk, rv])
    near = lax.ppermute(kv, "x", [(0, 1), (1, 2), (2, 3)])
    far = lax.ppermute(kv, "x", [(0, 2), (1, 3)])

    mine = jnp.stack([pk, pv])
    rows = lax.all_to_all(jnp.broadcast_to(mine, (32, 2, 8, 256)), ("z", "y"), 0, 0)
    other = lax.ppermute(rows, "core", [(0, 1), (1, 0)])
    picked = []
    for r in range(2):
        a = lax.dynamic_slice_in_dim(rows, groups[r] * 8, 8, 0)
        b = lax.dynamic_slice_in_dim(other, groups[r] * 8, 8, 0)
        even = jnp.where(core == 0, a, b)
        odd = jnp.where(core == 0, b, a)
        both = jnp.stack([even, odd], axis=1)
        picked.append(both.transpose(2, 0, 1, 3, 4).reshape(2, BLK, 256))
    own_prompts = jnp.stack(picked)
    slots = [own_prompts] + [shift(own_prompts, "x", N_X, d) for d in range(1, N_X)]

    carried = None
    sent_back = []
    for d in (0, 1, 3, 2):
        head = 2 * ((x - d) % N_X)
        scalars = jnp.stack([head, x, border]).astype(jnp.int32)
        *carried, grad_prompts = attend(scalars, q, do, rk, rv, near, far, slots[d], carried)
        sent_back.append(grad_prompts if d == 0 else shift(grad_prompts, "x", N_X, -d))
    out_q, own, grad_near, grad_far = carried
    back_near = lax.ppermute(grad_near, "x", [(1, 0), (2, 1), (3, 2)])
    back_far = lax.ppermute(grad_far, "x", [(2, 0), (3, 1)])

    summed = sum(part.astype(f32) for part in sent_back)
    dense = jnp.stack(
        [sum(jnp.where(groups[r] == g, summed[r], 0.0) for r in range(2)) for g in range(4)]
    )
    dense = dense.reshape(4, 2, 8, 2, 8, 256).transpose(3, 0, 2, 1, 4, 5)
    dense = dense.reshape(2, 32, 2, 8, 256).astype(bf16)
    keep = lax.dynamic_index_in_dim(dense, core, 0, keepdims=False)
    give = lax.dynamic_index_in_dim(dense, 1 - core, 0, keepdims=False)
    got = lax.ppermute(give, "core", [(0, 1), (1, 0)])
    half = (keep.astype(f32) + got.astype(f32)).astype(bf16)
    spread = lax.all_to_all(half, ("z", "y"), 0, 0)
    out_p = jnp.sum(spread.astype(f32), axis=0)

    out_kv = (own + (back_near.astype(f32) + back_far.astype(f32))).astype(bf16)
    return out_q, out_kv[0], out_kv[1], out_p[0], out_p[1]


def solution(mesh):
    fine = Mesh(mesh.devices.reshape(8, 4, 2, 4), ("z", "y", "core", "x"))
    dp = ("z", "y", "core")
    tokens = P(dp + ("x",), None)
    heads = P(dp, "x")
    per_dp = P(dp, None)
    return jax.shard_map(
        on_device,
        mesh=fine,
        in_specs=(tokens, tokens, tokens, tokens, heads, heads, per_dp, per_dp),
        out_specs=(tokens, tokens, tokens, heads, heads),
        check_vma=False,
    )
```

time: 607 us -> 125 us (0.21)
  the two profiles are of different devices: /device:TPU:1 before, /device:TPU:4 now
where the time goes in v1:
time: 125 us; the launch traced here: 123 us
  starting transfers between devices  39.7 us (32%)
  Pallas kernels  30.2 us (24%)
  waiting for transfers between devices  25.4 us (20%)
  local copies, waits for them, and re-layouts  10.5 us (8%)
  other arithmetic  10.3 us (8%)
  between operations  7.22 us (6%)
    pallas_call x4, Pallas kernels, attend(): pl.pallas_call(attention_kernel, out_shape=out_shape, grid_spec=pltpu.Pre...  30.2 us
    all_to_all x1, starting transfers between devices, on_device(): lax.all_to_all(jnp.broadcast_to(mine, (32, 2, 8, 256)), ('z', 'y'), 0, 0)  11.6 us
    all_to_all x1, starting transfers between devices, on_device(): spread = lax.all_to_all(half, ('z', 'y'), 0, 0)  9.72 us
    all_to_all x1, waiting for transfers between devices, on_device(): spread = lax.all_to_all(half, ('z', 'y'), 0, 0)  8.36 us
    ppermute x1, waiting for transfers between devices, on_device(): far = lax.ppermute(kv, 'x', [(0, 2), (1, 3)])  7.42 us
    unnamed x24, local copies, waits for them, and re-layouts  6.92 us
    ppermute x1, starting transfers between devices, on_device(): back_far = lax.ppermute(grad_far, 'x', [(2, 0), (3, 1)])  6.67 us
    ppermute x6, starting transfers between devices, shift(): return lax.ppermute(a, axis, [(i, (i + by) % size) for i in range(size)])  5.27 us
  transfers between devices with their start and end apart: 14, of which 5 were waited for; matrix products, arithmetic and copies ran while one was open for 9% of the time, Pallas kernels for 18%

profile of v1, /device:TPU:4, one launch (start us, length us, event | category | flops | bytes accessed | tf_op | source)
XLA Modules:
  0.0 123.3 jit_solution(16446161070829234645)
XLA Ops:
  0.7 0.9 pad_maximum_fusion.3
  2.2 11.6 %all-to-all-start = ((bf16[32,2,8,256]{3,2,1,0:T(8,128)(2,1)}), bf16[32,2,8,256]{3,2,1,0:T(8,128)(2,1)}, u32[]{:S(2)}, u32[]{:S(2)}) async-start(bf16[32,2,8,256]{3,2,1,0:T(8,128)(2,1)} %broadcast_in_dim.14), calls=%async_computation | async-start | bytes 524288 | tf_op jit(solution)/shard_map/all_to_all | solution.py:175
  13.9 1.9 %pad_maximum_fusion = bf16[2,128,1024]{2,1,0:T(8,128)(2,1)} fusion(bf16[1,128,1024]{2,1,0:T(8,128)(2,1)} %bitcast.55, bf16[1,128,1024]{2,1,0:T(8,128)(2,1)} %bitcast.54), kind=kLoop, calls=%fused_computation.1 | loop fusion | flops 262144 | bytes 1048576 | tf_op jit(solution)/shard_map/stack | solution.py:170
  15.7 3.1 %collective-permute-start = (bf16[2,128,1024]{2,1,0:T(8,128)(2,1)}, bf16[2,128,1024]{2,1,0:T(8,128)(2,1)S(1)}, u32[]{:S(2)}, u32[]{:S(2)}) collective-permute-start(bf16[2,128,1024]{2,1,0:T(8,128)(2,1)} %pad_maximum_fusion), channel_id=1, source_target_pairs={{0,1},{1,2},{2,3},{4,5},{5,6},{6,7},{8,9},{9,10},{10,11},{12,13},{... | collective-permute-start | bytes 1572872 | tf_op jit(solution)/shard_map/ppermute | solution.py:171
  18.8 1.3 %collective-permute-start.1 = (bf16[2,128,1024]{2,1,0:T(8,128)(2,1)}, bf16[2,128,1024]{2,1,0:T(8,128)(2,1)S(1)}, u32[]{:S(2)}, u32[]{:S(2)}) collective-permute-start(bf16[2,128,1024]{2,1,0:T(8,128)(2,1)} %pad_maximum_fusion), channel_id=1, source_target_pairs={{0,2},{1,3},{4,6},{5,7},{8,10},{9,11},{12,14},{13,15},{16,18},{17,... | collective-permute-start | bytes 1572872 | tf_op jit(solution)/shard_map/ppermute | solution.py:172
  20.2 1.3 %fusion.1 = s32[]{:T(128)} fusion(s32[1,512]{1,0:T(1,128)} %param.14), kind=kLoop, calls=%fused_computation.25 | loop fusion | flops 1535 | bytes 2052 | tf_op jit(solution)/shard_map/reduce_sum | solution.py:168
  22.2 4.3 %all-to-all-done = bf16[32,2,8,256]{3,2,1,0:T(8,128)(2,1)} async-done(((bf16[32,2,8,256]{3,2,1,0:T(8,128)(2,1)}), bf16[32,2,8,256]{3,2,1,0:T(8,128)(2,1)}, u32[]{:S(2)}, u32[]{:S(2)}) %all-to-all-start) | async-done | bytes 262176 | tf_op jit(solution)/shard_map/all_to_all | solution.py:175
  27.2 1.3 %fusion.2 = (s32[1,1]{1,0:T(1,128)}, s32[1,1]{1,0:T(1,128)}) fusion(s32[1,2]{1,0:T(1,128)} %param.15), kind=kLoop, calls=%fused_computation.30 | loop fusion | bytes 16 | tf_op jit(solution)/shard_map/slice | solution.py:179
  30.6 1.0 select_bitcast_fusion.3
  31.7 1.3 %collective-permute-start.5 = (bf16[2,2,128,256]{3,2,1,0:T(8,128)(2,1)S(1)}, bf16[2,2,128,256]{3,2,1,0:T(8,128)(2,1)S(1)}, u32[]{:S(2)}, u32[]{:S(2)}) collective-permute-start(bf16[2,2,128,256]{3,2,1,0:T(8,128)(2,1)S(1)} %pad_maximum_fusion.2.pr_ref), channel_id=1, source_target_pairs={{0,1},{1,2},{2,3},{3,0},{4,5},{5,6},{6,7},{7,4},{8,9},{9,10},{10,1... | collective-permute-start | bytes 786440 | tf_op jit(solution)/shard_map/ppermute | solution.py:161
  33.7 0.8 collective-permute-start.3
  34.5 1.1 collective-permute-start.4
  35.7 0.8 copy-done.2
  36.5 7.4 %collective-permute-done.1.far_ref = bf16[2,128,1024]{2,1,0:T(8,128)(2,1)S(1)} collective-permute-done((bf16[2,128,1024]{2,1,0:T(8,128)(2,1)}, bf16[2,128,1024]{2,1,0:T(8,128)(2,1)S(1)}, u32[]{:S(2)}, u32[]{:S(2)}) %collective-permute-start.1) | collective-permute-done | bytes 524320 | tf_op jit(solution)/shard_map/ppermute | solution.py:172
  44.7 1.6 %copy-done.1 = bf16[128,8192]{1,0:T(8,128)(2,1)S(1)} copy-done((bf16[128,8192]{1,0:T(8,128)(2,1)S(1)}, bf16[128,8192]{1,0:T(8,128)(2,1)}, u32[]{:S(2)}) %copy-start.1) | copy-done | bytes 2097176
  46.3 1.0 copy-done.3
  47.4 1.0 copy-done.6
  48.4 7.5 %shard_map.119 = (bf16[128,8192]{1,0:T(8,128)(2,1)}, f32[2,128,1024]{2,1,0:T(8,128)S(1)}, bf16[2,128,1024]{2,1,0:T(8,128)(2,1)S(1)}, bf16[2,128,1024]{2,1,0:T(8,128)(2,1)S(1)}, bf16[2,2,128,256]{3,2,1,0:T(8,128)(2,1)S(1)}) custom-call(s32[3]{0:T(128)S(1)} %add_add_fusion.3.sc_ref, bf16[128,8192]{1,0:T(8,128)(2,1)S(1)} %copy-done, ...), custom_call_target="tpu_custom_call" | custom-call | flops 2684354560 | bytes 4194304 | tf_op jit(solution)/shard_map/pallas_call | solution.py:143
  55.9 7.6 %shard_map.120 = (bf16[128,8192]{1,0:T(8,128)(2,1)}, f32[2,128,1024]{2,1,0:T(8,128)S(1)}, bf16[2,128,1024]{2,1,0:T(8,128)(2,1)S(1)}, bf16[2,128,1024]{2,1,0:T(8,128)(2,1)S(1)}, bf16[2,2,128,256]{3,2,1,0:T(8,128)(2,1)}) custom-call(s32[3]{0:T(128)S(1)} %add_add_fusion.2.sc_ref, ...), custom_call_target="tpu_custom_call", output_to_operand_aliasing={{0}: (8, {}), {1}: (9, {}), {2}: (10, {}), {3}: (11, {})} | custom-call | flops 2684354560 | bytes 4194304 | tf_op jit(solution)/shard_map/pallas_call | solution.py:143
  63.5 7.6 %shard_map.121 = (bf16[128,8192]{1,0:T(8,128)(2,1)}, f32[2,128,1024]{2,1,0:T(8,128)S(1)}, bf16[2,128,1024]{2,1,0:T(8,128)(2,1)S(1)}, bf16[2,128,1024]{2,1,0:T(8,128)(2,1)S(1)}, bf16[2,2,128,256]{3,2,1,0:T(8,128)(2,1)}) custom-call(s32[3]{0:T(128)S(1)} %add_add_fusion.1.sc_ref, ...), custom_call_target="tpu_custom_call", output_to_operand_aliasing={{0}: (8, {}), {1}: (9, {}), {2}: (10, {}), {3}: (11, {})} | custom-call | flops 2684354560 | bytes 4194304 | tf_op jit(solution)/shard_map/pallas_call | solution.py:143
  71.0 7.6 %shard_map.122 = (bf16[128,8192]{1,0:T(8,128)(2,1)}, f32[2,128,1024]{2,1,0:T(8,128)S(1)}, bf16[2,128,1024]{2,1,0:T(8,128)(2,1)S(1)}, bf16[2,128,1024]{2,1,0:T(8,128)(2,1)S(1)}, bf16[2,2,128,256]{3,2,1,0:T(8,128)(2,1)}) custom-call(s32[3]{0:T(128)S(1)} %add_add_fusion.sc_ref, ...), custom_call_target="tpu_custom_call", output_to_operand_aliasing={{0}: (8, {}), {1}: (9, {}), {2}: (10, {}), {3}: (11, {})} | custom-call | flops 2684354560 | bytes 4194304 | tf_op jit(solution)/shard_map/pallas_call | solution.py:143
  78.6 0.8 copy-done.7
  79.4 0.8 copy-done.8
  80.2 2.0 %collective-permute-start.8 = (bf16[2,2,128,256]{3,2,1,0:T(8,128)(2,1)}, bf16[2,2,128,256]{3,2,1,0:T(8,128)(2,1)S(1)}, u32[]{:S(2)}, u32[]{:S(2)}) collective-permute-start(bf16[2,2,128,256]{3,2,1,0:T(8,128)(2,1)} %get-tuple-element.42), channel_id=1, source_target_pairs={{0,3},{1,0},{2,1},{3,2},{4,7},{5,4},{6,5},{7,6},{8,11},{9,8},{10,9... | collective-permute-start | bytes 786440 | tf_op jit(solution)/shard_map/ppermute | solution.py:161
  87.3 6.7 %collective-permute-start.7 = (bf16[2,128,1024]{2,1,0:T(8,128)(2,1)}, bf16[2,128,1024]{2,1,0:T(8,128)(2,1)S(1)}, u32[]{:S(2)}, u32[]{:S(2)}) collective-permute-start(bf16[2,128,1024]{2,1,0:T(8,128)(2,1)} %copy-done.8), channel_id=1, source_target_pairs={{2,0},{3,1},{6,4},{7,5},{10,8},{11,9},{14,12},{15,13},{18,16},{19,... | collective-permute-start | bytes 1572872 | tf_op jit(solution)/shard_map/ppermute | solution.py:197
  94.0 1.9 %collective-permute-start.6 = (bf16[2,128,1024]{2,1,0:T(8,128)(2,1)}, bf16[2,128,1024]{2,1,0:T(8,128)(2,1)S(1)}, u32[]{:S(2)}, u32[]{:S(2)}) collective-permute-start(bf16[2,128,1024]{2,1,0:T(8,128)(2,1)} %copy-done.7), channel_id=1, source_target_pairs={{1,0},{2,1},{3,2},{5,4},{6,5},{7,6},{9,8},{10,9},{11,10},{13,12},{... | collective-permute-start | bytes 1572872 | tf_op jit(solution)/shard_map/ppermute | solution.py:196
  95.9 1.1 convert_add_fusion.1
  97.4 1.5 %collective-permute-done.11 = bf16[32,2,8,256]{3,2,1,0:T(8,128)(2,1)S(1)} collective-permute-done((bf16[32,2,8,256]{3,2,1,0:T(8,128)(2,1)S(1)}, bf16[32,2,8,256]{3,2,1,0:T(8,128)(2,1)S(1)}, u32[]{:S(2)}, u32[]{:S(2)}) %collective-permute-start.11) | collective-permute-done | bytes 262176 | tf_op jit(solution)/shard_map/ppermute | solution.py:207
  99.7 9.7 %all-to-all-start.1 = ((bf16[32,2,8,256]{3,2,1,0:T(8,128)(2,1)}), bf16[32,2,8,256]{3,2,1,0:T(8,128)(2,1)S(1)}, u32[]{:S(2)}, u32[]{:S(2)}) async-start(bf16[32,2,8,256]{3,2,1,0:T(8,128)(2,1)} %fusion), calls=%async_computation.1 | async-start | bytes 524288 | tf_op jit(solution)/shard_map/all_to_all | solution.py:209
  109.4 3.8 %collective-permute-done.6 = bf16[2,128,1024]{2,1,0:T(8,128)(2,1)S(1)} collective-permute-done((bf16[2,128,1024]{2,1,0:T(8,128)(2,1)}, bf16[2,128,1024]{2,1,0:T(8,128)(2,1)S(1)}, u32[]{:S(2)}, u32[]{:S(2)}) %collective-permute-start.6) | collective-permute-done | bytes 524320 | tf_op jit(solution)/shard_map/ppermute | solution.py:196
  113.5 0.8 slice_bitcast_fusion
  114.3 8.4 %all-to-all-done.1 = bf16[32,2,8,256]{3,2,1,0:T(8,128)(2,1)S(1)} async-done(((bf16[32,2,8,256]{3,2,1,0:T(8,128)(2,1)}), bf16[32,2,8,256]{3,2,1,0:T(8,128)(2,1)S(1)}, u32[]{:S(2)}, u32[]{:S(2)}) %all-to-all-start.1) | async-done | bytes 262176 | tf_op jit(solution)/shard_map/all_to_all | solution.py:209
  (48 shorter events, 6.6 us)
Async XLA Ops:
  0.6 44.1 %copy-start.9 = (bf16[128,1024]{1,0:T(8,128)(2,1)S(1)}, bf16[128,1024]{1,0:T(8,128)(2,1)}, u32[]{:S(2)}) copy-start(bf16[128,1024]{1,0:T(8,128)(2,1)} %ko_ref.7) | copy-start | bytes 786436
  0.6 44.1 %copy-start = (bf16[128,8192]{1,0:T(8,128)(2,1)S(1)}, bf16[128,8192]{1,0:T(8,128)(2,1)}, u32[]{:S(2)}) copy-start(bf16[128,8192]{1,0:T(8,128)(2,1)} %q_ref.7) | copy-start | bytes 6291460
  2.2 24.3 %all-to-all-start = ((bf16[32,2,8,256]{3,2,1,0:T(8,128)(2,1)}), bf16[32,2,8,256]{3,2,1,0:T(8,128)(2,1)}, u32[]{:S(2)}, u32[]{:S(2)}) async-start(bf16[32,2,8,256]{3,2,1,0:T(8,128)(2,1)} %broadcast_in_dim.14), calls=%async_computation | async-start | bytes 524288 | tf_op jit(solution)/shard_map/all_to_all | solution.py:175
  15.7 20.0 %collective-permute-start = (bf16[2,128,1024]{2,1,0:T(8,128)(2,1)}, bf16[2,128,1024]{2,1,0:T(8,128)(2,1)S(1)}, u32[]{:S(2)}, u32[]{:S(2)}) collective-permute-start(bf16[2,128,1024]{2,1,0:T(8,128)(2,1)} %pad_maximum_fusion), channel_id=1, source_target_pairs={{0,1},{1,2},{2,3},{4,5},{5,6},{6,7},{8,9},{9,10},{10,11},{12,13},{... | collective-permute-start | bytes 1572872 | tf_op jit(solution)/shard_map/ppermute | solution.py:171
  18.8 25.1 %collective-permute-start.1 = (bf16[2,128,1024]{2,1,0:T(8,128)(2,1)}, bf16[2,128,1024]{2,1,0:T(8,128)(2,1)S(1)}, u32[]{:S(2)}, u32[]{:S(2)}) collective-permute-start(bf16[2,128,1024]{2,1,0:T(8,128)(2,1)} %pad_maximum_fusion), channel_id=1, source_target_pairs={{0,2},{1,3},{4,6},{5,7},{8,10},{9,11},{12,14},{13,15},{16,18},{17,... | collective-permute-start | bytes 1572872 | tf_op jit(solution)/shard_map/ppermute | solution.py:172
  26.5 4.1 %collective-permute-start.2 = (bf16[32,2,8,256]{3,2,1,0:T(8,128)(2,1)}, bf16[32,2,8,256]{3,2,1,0:T(8,128)(2,1)}, u32[]{:S(2)}, u32[]{:S(2)}) collective-permute-start(bf16[32,2,8,256]{3,2,1,0:T(8,128)(2,1)} %all-to-all-done), channel_id=1, source_target_pairs={{0,4},{4,0},{1,5},{5,1},{2,6},{6,2},{3,7},{7,3},{8,12},{12,8},{9,1... | collective-permute-start | bytes 786440 | tf_op jit(solution)/shard_map/ppermute | solution.py:176
  30.6 14.1 %copy-start.10 = (bf16[128,1024]{1,0:T(8,128)(2,1)S(1)}, bf16[128,1024]{1,0:T(8,128)(2,1)}, u32[]{:S(2)}) copy-start(bf16[128,1024]{1,0:T(8,128)(2,1)} %vo_ref.7) | copy-start | bytes 786436
  31.7 24.2 %collective-permute-start.5 = (bf16[2,2,128,256]{3,2,1,0:T(8,128)(2,1)S(1)}, bf16[2,2,128,256]{3,2,1,0:T(8,128)(2,1)S(1)}, u32[]{:S(2)}, u32[]{:S(2)}) collective-permute-start(bf16[2,2,128,256]{3,2,1,0:T(8,128)(2,1)S(1)} %pad_maximum_fusion.2.pr_ref), channel_id=1, source_target_pairs={{0,1},{1,2},{2,3},{3,0},{4,5},{5,6},{6,7},{7,4},{8,9},{9,10},{10,1... | collective-permute-start | bytes 786440 | tf_op jit(solution)/shard_map/ppermute | solution.py:161
  33.7 37.3 %collective-permute-start.3 = (bf16[2,2,128,256]{3,2,1,0:T(8,128)(2,1)S(1)}, bf16[2,2,128,256]{3,2,1,0:T(8,128)(2,1)S(1)}, u32[]{:S(2)}, u32[]{:S(2)}) collective-permute-start(bf16[2,2,128,256]{3,2,1,0:T(8,128)(2,1)S(1)} %pad_maximum_fusion.2.pr_ref), channel_id=1, source_target_pairs={{0,2},{1,3},{2,0},{3,1},{4,6},{5,7},{6,4},{7,5},{8,10},{9,11},{10,... | collective-permute-start | bytes 786440 | tf_op jit(solution)/shard_map/ppermute | solution.py:161
  34.5 28.9 %collective-permute-start.4 = (bf16[2,2,128,256]{3,2,1,0:T(8,128)(2,1)S(1)}, bf16[2,2,128,256]{3,2,1,0:T(8,128)(2,1)S(1)}, u32[]{:S(2)}, u32[]{:S(2)}) collective-permute-start(bf16[2,2,128,256]{3,2,1,0:T(8,128)(2,1)S(1)} %pad_maximum_fusion.2.pr_ref), channel_id=1, source_target_pairs={{0,3},{1,0},{2,1},{3,2},{4,7},{5,4},{6,5},{7,6},{8,11},{9,8},{10,9... | collective-permute-start | bytes 786440 | tf_op jit(solution)/shard_map/ppermute | solution.py:161
  35.7 0.8 copy-start.2
  43.9 0.8 copy-start.5
  44.7 1.6 %copy-start.1 = (bf16[128,8192]{1,0:T(8,128)(2,1)S(1)}, bf16[128,8192]{1,0:T(8,128)(2,1)}, u32[]{:S(2)}) copy-start(bf16[128,8192]{1,0:T(8,128)(2,1)} %do_ref.7) | copy-start | bytes 6291460
  46.3 1.0 copy-start.3
  47.4 1.0 copy-start.6
  48.4 7.5 %copy-start.4 = (bf16[2,128,1024]{2,1,0:T(8,128)(2,1)S(1)}, bf16[2,128,1024]{2,1,0:T(8,128)(2,1)}, u32[]{:S(2)}) copy-start(bf16[2,128,1024]{2,1,0:T(8,128)(2,1)} %copy-done.2) | copy-start | bytes 1572868
  55.9 7.6 %copy-start.11 = (bf16[2,2,128,256]{3,2,1,0:T(8,128)(2,1)}, bf16[2,2,128,256]{3,2,1,0:T(8,128)(2,1)S(1)}, u32[]{:S(2)}) copy-start(bf16[2,2,128,256]{3,2,1,0:T(8,128)(2,1)S(1)} %get-tuple-element.41) | copy-start | bytes 786436
  78.6 0.8 copy-start.7
  79.4 0.8 copy-start.8
  80.2 15.7 %collective-permute-start.10 = (bf16[2,2,128,256]{3,2,1,0:T(8,128)(2,1)}, bf16[2,2,128,256]{3,2,1,0:T(8,128)(2,1)S(1)}, u32[]{:S(2)}, u32[]{:S(2)}) collective-permute-start(bf16[2,2,128,256]{3,2,1,0:T(8,128)(2,1)} %get-tuple-element.44), channel_id=1, source_target_pairs={{0,2},{1,3},{2,0},{3,1},{4,6},{5,7},{6,4},{7,5},{8,10},{9,11},{10,... | collective-permute-start | bytes 786440 | tf_op jit(solution)/shard_map/ppermute | solution.py:161
  80.2 15.7 %collective-permute-start.9 = (bf16[2,2,128,256]{3,2,1,0:T(8,128)(2,1)}, bf16[2,2,128,256]{3,2,1,0:T(8,128)(2,1)S(1)}, u32[]{:S(2)}, u32[]{:S(2)}) collective-permute-start(bf16[2,2,128,256]{3,2,1,0:T(8,128)(2,1)} %get-tuple-element.43), channel_id=1, source_target_pairs={{0,1},{1,2},{2,3},{3,0},{4,5},{5,6},{6,7},{7,4},{8,9},{9,10},{10,1... | collective-permute-start | bytes 786440 | tf_op jit(solution)/shard_map/ppermute | solution.py:161
  80.2 15.7 %collective-permute-start.8 = (bf16[2,2,128,256]{3,2,1,0:T(8,128)(2,1)}, bf16[2,2,128,256]{3,2,1,0:T(8,128)(2,1)S(1)}, u32[]{:S(2)}, u32[]{:S(2)}) collective-permute-start(bf16[2,2,128,256]{3,2,1,0:T(8,128)(2,1)} %get-tuple-element.42), channel_id=1, source_target_pairs={{0,3},{1,0},{2,1},{3,2},{4,7},{5,4},{6,5},{7,6},{8,11},{9,8},{10,9... | collective-permute-start | bytes 786440 | tf_op jit(solution)/shard_map/ppermute | solution.py:161
  87.3 22.1 %collective-permute-start.7 = (bf16[2,128,1024]{2,1,0:T(8,128)(2,1)}, bf16[2,128,1024]{2,1,0:T(8,128)(2,1)S(1)}, u32[]{:S(2)}, u32[]{:S(2)}) collective-permute-start(bf16[2,128,1024]{2,1,0:T(8,128)(2,1)} %copy-done.8), channel_id=1, source_target_pairs={{2,0},{3,1},{6,4},{7,5},{10,8},{11,9},{14,12},{15,13},{18,16},{19,... | collective-permute-start | bytes 1572872 | tf_op jit(solution)/shard_map/ppermute | solution.py:197
  94.0 19.3 %collective-permute-start.6 = (bf16[2,128,1024]{2,1,0:T(8,128)(2,1)}, bf16[2,128,1024]{2,1,0:T(8,128)(2,1)S(1)}, u32[]{:S(2)}, u32[]{:S(2)}) collective-permute-start(bf16[2,128,1024]{2,1,0:T(8,128)(2,1)} %copy-done.7), channel_id=1, source_target_pairs={{1,0},{2,1},{3,2},{5,4},{6,5},{7,6},{9,8},{10,9},{11,10},{13,12},{... | collective-permute-start | bytes 1572872 | tf_op jit(solution)/shard_map/ppermute | solution.py:196
  97.3 1.6 %collective-permute-start.11 = (bf16[32,2,8,256]{3,2,1,0:T(8,128)(2,1)S(1)}, bf16[32,2,8,256]{3,2,1,0:T(8,128)(2,1)S(1)}, u32[]{:S(2)}, u32[]{:S(2)}) collective-permute-start(bf16[32,2,8,256]{3,2,1,0:T(8,128)(2,1)S(1)} %dynamic-slice_bitcast_fusion), channel_id=1, source_target_pairs={{0,4},{4,0},{1,5},{5,1},{2,6},{6,2},{3,7},{7,3},{8,12},{12,8},{9,1... | collective-permute-start | bytes 786440 | tf_op jit(solution)/shard_map/ppermute | solution.py:207
  99.7 23.0 %all-to-all-start.1 = ((bf16[32,2,8,256]{3,2,1,0:T(8,128)(2,1)}), bf16[32,2,8,256]{3,2,1,0:T(8,128)(2,1)S(1)}, u32[]{:S(2)}, u32[]{:S(2)}) async-start(bf16[32,2,8,256]{3,2,1,0:T(8,128)(2,1)} %fusion), calls=%async_computation.1 | async-start | bytes 524288 | tf_op jit(solution)/shard_map/all_to_all | solution.py:209

commit v2 on v1

v2 whole, which is shorter than its diff:
```python
import functools
import functools
import math

import jax
import jax.numpy as jnp
from jax import lax
from jax.experimental import pallas as pl
from jax.experimental.pallas import tpu as pltpu
from jax.sharding import Mesh, PartitionSpec as P

HD = 128
BLK = 128
HEAD_COLS = 1024
KV_HEADS = 8
N_X = 4
FACTOR = HD**-0.5
LOG2_SCALE = FACTOR * math.log2(math.e)
NEG = -1e30
HEADS_STEP = 2
LANES = HEADS_STEP * BLK
STEPS = 4
bf16, f32 = jnp.bfloat16, jnp.float32


def dot_nt(a, b):
    return lax.dot_general(a, b, (((1,), (1,)), ((), ())), preferred_element_type=f32)


def dot_nn(a, b):
    return lax.dot_general(a, b, (((1,), (0,)), ((), ())), preferred_element_type=f32)


def fold(x, op):
    parts=[x[8*i:8*i+8] for i in range(x.shape[0]//8)]
    while len(parts)>1:
        parts=[op(parts[i],parts[i+1]) if i+1<len(parts) else parts[i] for i in range(0,len(parts),2)]
    return parts[0]
def attention_kernel(
    slot, sc_ref, seg_ref, q_ref, do_ref, kv_ref, near_ref, far_ref, pr_ref, *refs):
    dq_ref, own_ref, dnear_ref, dfar_ref, dpr_ref = refs[-18:-13]
    bias, e0,e1,g0,g1,p0,p1,d0,d1,dkacc,dvacc,dkpacc,dvpacc = refs[-13:]
    ebuf,gbuf,pbuf,dsbuf=(e0,e1),(g0,g1),(p0,p1),(d0,d1)
    place = sc_ref[0]
    border = jnp.sum((seg_ref[...] == 0).astype(jnp.int32), axis=1, keepdims=True)
    u = lax.broadcasted_iota(jnp.int32,(3*BLK,BLK),0)+(place-2)*BLK
    t = lax.broadcasted_iota(jnp.int32,(3*BLK,BLK),1)+place*BLK
    ok=(u>=0)&(u<=t)&((u>=border)==(t>=border))

    @pl.when(pl.program_id(0) == 0)
    def _():
        bias[...] = jnp.where(ok, 0.0, NEG).astype(f32)

    row_t = lax.broadcasted_iota(jnp.int32,(BLK,HD),0)+place*BLK
    first=jnp.where(row_t<border,1.0,0.0).astype(bf16)
    second=jnp.where(row_t<border,0.0,1.0).astype(bf16)
    first=jnp.concatenate([first]*HEADS_STEP,axis=0); second=jnp.concatenate([second]*HEADS_STEP,axis=0)
    lane_t=lax.broadcasted_iota(jnp.int32,(HD,BLK),1)+place*BLK
    lane_first=jnp.where(lane_t<border,1.0,0.0).astype(bf16)
    lane_first=jnp.concatenate([lane_first]*HEADS_STEP,axis=1)
    lane_second=1-lane_first
    k_p=jnp.concatenate([pr_ref[0,0],pr_ref[1,0]],axis=1)
    v_p=jnp.concatenate([pr_ref[0,1],pr_ref[1,1]],axis=1)
    ks=[k_p, far_ref[0],near_ref[0],kv_ref[0]]
    vs=[v_p, far_ref[1],near_ref[1],kv_ref[1]]
    k_r_t=jnp.concatenate(ks[1:],axis=0).T
    k_p_t=jnp.concatenate([pr_ref[0,0],pr_ref[1,0]],axis=0).T

    st={}
    def cols(pair,j): return pl.ds((HEADS_STEP*pair+j)*HD,HD)
    def load(p):
        q=jnp.concatenate([q_ref[:,cols(p,j)] for j in range(HEADS_STEP)],axis=0)
        do=jnp.concatenate([do_ref[:,cols(p,j)] for j in range(HEADS_STEP)],axis=0)
        return q,do
    def two(x): return jnp.concatenate([x*first,x*second],axis=1)
    def s_chunk(p,c):
        q,_=load(p)
        s=dot_nt(ks[c], two(q) if c==0 else q)
        if c>0:
            bc=bias[(c-1)*BLK:c*BLK]
            s=s+jnp.concatenate([bc]*HEADS_STEP,axis=1)
        ebuf[p%2][c*BLK:(c+1)*BLK]=s
        m=fold(s,jnp.maximum)
        st[p,"top"]=m if c==0 else jnp.maximum(st[p,"top"],m)
        if c==3: st[p,"top"]=jnp.max(st[p,"top"],axis=0,keepdims=True)
    def g_chunk(p,c):
        _,do=load(p)
        gbuf[p%2][c*BLK:(c+1)*BLK]=dot_nt(vs[c], two(do) if c==0 else do)
    def pass2(p,c):
        sl=slice(c*BLK,(c+1)*BLK)
        e=jnp.exp2((ebuf[p%2][sl]-st[p,"top"])*LOG2_SCALE)
        ebuf[p%2][sl]=e
        a1=fold(e,jnp.add); a2=fold(e*gbuf[p%2][sl],jnp.add)
        st[p,"tot"]=a1 if c==0 else st[p,"tot"]+a1
        st[p,"dl"]=a2 if c==0 else st[p,"dl"]+a2
        if c==3:
            st[p,"inv"]=1.0/jnp.sum(st[p,"tot"],axis=0,keepdims=True)
            st[p,"delta"]=jnp.sum(st[p,"dl"],axis=0,keepdims=True)*st[p,"inv"]
    def pass3(p,c):
        sl=slice(c*BLK,(c+1)*BLK)
        w=ebuf[p%2][sl]*st[p,"inv"]
        pbuf[p%2][sl]=w.astype(bf16)
        dsbuf[p%2][sl]=(w*(gbuf[p%2][sl]-st[p,"delta"])).astype(bf16)
    def dq_part(p):
        ds_p=dsbuf[p%2][:BLK]
        ds_two=jnp.concatenate([ds_p*lane_first,ds_p*lane_second],axis=0)
        dq_t=dot_nn(k_r_t,dsbuf[p%2][BLK:])+dot_nn(k_p_t,ds_two)
        dq=(dq_t*FACTOR).T.astype(bf16)
        for j in range(HEADS_STEP):
            dq_ref[:,cols(p,j)]=dq[j*BLK:(j+1)*BLK]
    def dk_part(p,c,kv):
        x=load(p)[kv]
        src=(dsbuf,pbuf)[kv][p%2][c*BLK:(c+1)*BLK]
        r=dot_nn(src, two(x) if c==0 else x)
        acc=(dkacc,dvacc)[kv] if c>0 else (dkpacc,dvpacc)[kv]
        sl=slice((c-1)*BLK,c*BLK) if c>0 else slice(0,BLK)
        if p==0: acc[sl]=r
        else: acc[sl]=acc[sl]+r
    def mk(p):
        l=[]
        for c in range(4):
            l.append(lambda c=c: s_chunk(p,c))
        for c in range(4):
            l.append(lambda c=c: g_chunk(p,c))
        return l
    def md(p):
        l=[lambda: dq_part(p)]
        for kv in range(2):
            for c in range(4): l.append(lambda c=c,kv=kv: dk_part(p,c,kv))
        return l
    def vp(p):
        return [lambda c=c: pass2(p,c) for c in range(4)]+[lambda c=c: pass3(p,c) for c in range(4)]
    def weave(v,m):
        n=max(len(v),1)
        for i in range(n):
            for f in m[len(m)*i//n:len(m)*(i+1)//n]: f()
            if i<len(v): v[i]()
    for f in mk(0): f()
    for p in range(STEPS):
        m=[]
        if p>0: m+=md(p-1)
        if p+1<STEPS: m+=mk(p+1)
        weave(vp(p),m)
    for f in md(STEPS-1): f()
    for j,(r,pp) in enumerate(((dkacc,dkpacc),(dvacc,dvpacc))):
        sc_=FACTOR if j==0 else 1.0
        dfar_ref[j]=(r[:BLK]*sc_).astype(bf16)
        dnear_ref[j]=(r[BLK:2*BLK]*sc_).astype(bf16)
        own_ref[j]=r[2*BLK:]*sc_
        dpr_ref[0,j]=(pp[:,:HD]*sc_).astype(bf16)
        dpr_ref[1,j]=(pp[:,HD:]*sc_).astype(bf16)

def attend(slot, place, seg, q, do, kv, near, far, prompts, carried):
    def head_of(i, sc):
        return 2 * lax.rem(sc[0] + (N_X - slot), N_X) + i

    def at_head(i, sc):
        return (0, head_of(i, sc))

    def pair_at_head(i, sc):
        return (0, 0, head_of(i, sc))

    wide_spec = pl.BlockSpec((BLK, HEAD_COLS), at_head)
    one_spec = pl.BlockSpec((BLK, HD), at_head)
    pair_spec = pl.BlockSpec((2, BLK, HD), pair_at_head)
    prompt_spec = pl.BlockSpec((2, 2, BLK, HD), lambda i, sc: (0, 0, 0, i))
    seg_spec = pl.BlockSpec((1, 512), lambda i, sc: (0, 0))
    out_shape = (
        jax.ShapeDtypeStruct((BLK, KV_HEADS * HEAD_COLS), bf16),
        jax.ShapeDtypeStruct((2, BLK, KV_HEADS * HD), f32),
        jax.ShapeDtypeStruct((2, BLK, KV_HEADS * HD), bf16),
        jax.ShapeDtypeStruct((2, BLK, KV_HEADS * HD), bf16),
        jax.ShapeDtypeStruct((2, 2, BLK, 2 * HD), bf16),
    )
    in_specs = [seg_spec, wide_spec, wide_spec, pair_spec, pair_spec, pair_spec, prompt_spec]
    aliases = {}
    operands = [seg, q, do, kv, near, far, prompts]
    if carried is not None:
        for k, array in enumerate(carried):
            aliases[1 + len(operands)] = k
            operands.append(array)
            in_specs.append(pl.BlockSpec(memory_space=pl.ANY))
    return pl.pallas_call(
        functools.partial(attention_kernel, slot),
        out_shape=out_shape,
        grid_spec=pltpu.PrefetchScalarGridSpec(
            num_scalar_prefetch=1,
            grid=(2,),
            in_specs=in_specs,
            out_specs=(wide_spec, pair_spec, pair_spec, pair_spec, prompt_spec),
            scratch_shapes=[pltpu.VMEM((3 * BLK, BLK), f32)]
            + [pltpu.VMEM((4 * BLK, LANES), f32)] * 4
            + [pltpu.VMEM((4 * BLK, LANES), bf16)] * 4
            + [pltpu.VMEM((3 * BLK, HD), f32)] * 2
            + [pltpu.VMEM((BLK, 2 * HD), f32)] * 2,
        ),
        input_output_aliases=aliases,
        compiler_params=pltpu.CompilerParams(vmem_limit_bytes=12 * 1024 * 1024),
        cost_estimate=pl.CostEstimate(
            flops=5 * 2 * 1024 * 512 * 128 * 2 * 2, bytes_accessed=4 << 20, transcendentals=1 << 20
        ),
    )(place, *operands)


def prepare_kernel(pk_ref, pv_ref, rk_ref, rv_ref, rows_ref, kv_ref):
    kv_ref[0] = rk_ref[...]
    kv_ref[1] = rv_ref[...]
    both = jnp.concatenate([pk_ref[...].astype(f32), pv_ref[...].astype(f32)], axis=0)
    both = both.astype(bf16)
    for i in range(32):
        rows_ref[i] = both


def prepare(pk, pv, rk, rv):
    return pl.pallas_call(
        prepare_kernel,
        out_shape=(
            jax.ShapeDtypeStruct((32, 16, 256), bf16),
            jax.ShapeDtypeStruct((2, BLK, KV_HEADS * HD), bf16),
        ),
        compiler_params=pltpu.CompilerParams(vmem_limit_bytes=56 * 1024 * 1024),
    )(pk, pv, rk, rv)


def pick_kernel(group_ref, core_ref, mine_ref, other_ref, near_ref, far_ref, out_ref):
    first_core = core_ref[0] == 0
    for r in range(2):
        start = group_ref[0, r] * 8
        for j in range(8):
            mine = mine_ref[start + j].astype(f32)
            other = other_ref[start + j].astype(f32)
            even = jnp.where(first_core, mine, other)
            odd = jnp.where(first_core, other, mine)
            for kv in range(2):
                rows = slice(8 * kv, 8 * kv + 8)
                out_ref[r, kv, 16 * j : 16 * j + 16, :] = jnp.concatenate(
                    [even[rows], odd[rows]], axis=0
                ).astype(bf16)


def pick(groups, core, mine, other, near, far):
    whole = pl.BlockSpec((32, 16, 256), lambda i, g, c: (0, 0, 0))
    return pl.pallas_call(
        pick_kernel,
        compiler_params=pltpu.CompilerParams(vmem_limit_bytes=6 * 1024 * 1024),
        out_shape=jax.ShapeDtypeStruct((2, 2, BLK, 256), bf16),
        grid_spec=pltpu.PrefetchScalarGridSpec(
            num_scalar_prefetch=2,
            grid=(1,),
            in_specs=[whole, whole] + [pl.BlockSpec(memory_space=pl.ANY)] * 2,
            out_specs=pl.BlockSpec((2, 2, BLK, 256), lambda i, g, c: (0, 0, 0, 0)),
        ),
    )(groups, core, mine, other, near, far)


def spread_kernel(group_ref, core_ref, a_ref, b_ref, c_ref, d_ref, keep_ref, give_ref):
    first_core = core_ref[0] == 0
    for j in range(8):
        rows = slice(16 * j, 16 * j + 16)
        total = []
        for r in range(2):
            total.append(
                [
                    (a_ref[r, kv, rows].astype(f32) + b_ref[r, kv, rows].astype(f32))
                    + (c_ref[r, kv, rows].astype(f32) + d_ref[r, kv, rows].astype(f32))
                    for kv in range(2)
                ]
            )
        for g in range(4):
            at = [
                jnp.where(group_ref[0, 0] == g, total[0][kv], 0.0)
                + jnp.where(group_ref[0, 1] == g, total[1][kv], 0.0)
                for kv in range(2)
            ]
            even = jnp.concatenate([at[0][:8], at[1][:8]], axis=0)
            odd = jnp.concatenate([at[0][8:], at[1][8:]], axis=0)
            keep_ref[8 * g + j] = jnp.where(first_core, even, odd)
            give_ref[8 * g + j] = jnp.where(first_core, odd, even).astype(bf16)


def spread(groups, core, parts):
    part = pl.BlockSpec((2, 2, BLK, 256), lambda i, g, c: (0, 0, 0, 0))
    whole = pl.BlockSpec((32, 16, 256), lambda i, g, c: (0, 0, 0))
    return pl.pallas_call(
        spread_kernel,
        compiler_params=pltpu.CompilerParams(vmem_limit_bytes=6 * 1024 * 1024),
        out_shape=(
            jax.ShapeDtypeStruct((32, 16, 256), f32),
            jax.ShapeDtypeStruct((32, 16, 256), bf16),
        ),
        grid_spec=pltpu.PrefetchScalarGridSpec(
            num_scalar_prefetch=2, grid=(1,), in_specs=[part] * 4, out_specs=(whole, whole)
        ),
    )(groups, core, *parts)


def shift(a, axis, size, by):
    return lax.ppermute(a, axis, [(i, (i + by) % size) for i in range(size)])


def on_device(q, rk, rv, do, pk, pv, segment_ids, response_group):
    place = lax.axis_index("x").astype(jnp.int32).reshape(1)
    core = lax.axis_index("core").astype(jnp.int32).reshape(1)

    sent, kv = prepare(pk, pv, rk, rv)
    near = lax.ppermute(kv, "x", [(0, 1), (1, 2), (2, 3)])
    far = lax.ppermute(kv, "x", [(0, 2), (1, 3)])

    rows = lax.all_to_all(sent, ("z", "y"), 0, 0)
    rows, near = lax.optimization_barrier((rows, near))
    other = lax.ppermute(rows, "core", [(0, 1), (1, 0)])
    own_prompts = pick(response_group, core, rows, other, near, far)
    slots = [own_prompts] + [shift(own_prompts, "x", N_X, d) for d in range(1, N_X)]

    carried = None
    sent_back = {}
    for d in (0, 1, 2, 3):
        prompts = slots[d]
        if d == 3:
            prompts, sent_back[1] = lax.optimization_barrier((prompts, sent_back[1]))
        *carried, grad_prompts = attend(
            d, place, segment_ids, q, do, kv, near, far, prompts, carried
        )
        sent_back[d] = grad_prompts if d == 0 else shift(grad_prompts, "x", N_X, -d)
    out_q, own, grad_near, grad_far = carried
    back_near = lax.ppermute(grad_near, "x", [(1, 0), (2, 1), (3, 2)])
    back_far = lax.ppermute(grad_far, "x", [(2, 0), (3, 1)])

    keep, give = spread(response_group, core, [sent_back[d] for d in range(N_X)])
    got = lax.ppermute(give, "core", [(0, 1), (1, 0)])
    half = (keep + got.astype(f32)).astype(bf16)
    spread_out = lax.all_to_all(half, ("z", "y"), 0, 0)
    out_p = jnp.sum(spread_out.astype(f32), axis=0)

    out_kv = (own + (back_near.astype(f32) + back_far.astype(f32))).astype(bf16)
    return out_q, out_kv[0], out_kv[1], out_p[:8], out_p[8:]


def solution(mesh):
    fine = Mesh(mesh.devices.reshape(8, 4, 2, 4), ("z", "y", "core", "x"))
    dp = ("z", "y", "core")
    tokens = P(dp + ("x",), None)
    heads = P(dp, "x")
    per_dp = P(dp, None)
    return jax.shard_map(
        on_device,
        mesh=fine,
        in_specs=(tokens, tokens, tokens, tokens, heads, heads, per_dp, per_dp),
        out_specs=(tokens, tokens, tokens, heads, heads),
        check_vma=False,
    )
```

time: 125 us -> 111 us (0.89)
  the two profiles are of different devices: /device:TPU:4 before, /device:TPU:1 now
where the time goes in v2:
time: 111 us; the launch traced here: 110 us
  starting transfers between devices  48.7 us (44%)
  Pallas kernels  30.1 us (27%)
  waiting for transfers between devices  22.8 us (21%)
  local copies, waits for them, and re-layouts  6.82 us (6%)
    pallas_call x4, Pallas kernels, attend(): pl.pallas_call(functools.partial(attention_kernel, slot), out_shape=out_s...  24.9 us
    all_to_all x1, starting transfers between devices, on_device(): rows = lax.all_to_all(sent, ('z', 'y'), 0, 0)  11.2 us
    all_to_all x1, waiting for transfers between devices, on_device(): spread_out = lax.all_to_all(half, ('z', 'y'), 0, 0)  10.5 us
    all_to_all x1, starting transfers between devices, on_device(): spread_out = lax.all_to_all(half, ('z', 'y'), 0, 0)  9.81 us
    ppermute x1, starting transfers between devices, on_device(): got = lax.ppermute(give, 'core', [(0, 1), (1, 0)])  7.09 us
    ppermute x6, starting transfers between devices, shift(): return lax.ppermute(a, axis, [(i, (i + by) % size) for i in range(size)])  6.58 us
    all_to_all x1, waiting for transfers between devices, on_device(): rows = lax.all_to_all(sent, ('z', 'y'), 0, 0)  6.3 us
    unnamed x20, local copies, waits for them, and re-layouts  5.38 us
  transfers between devices with their start and end apart: 14, of which 6 were waited for; matrix products, arithmetic and copies ran while one was open for 2% of the time, Pallas kernels for 23%

profile of v2, /device:TPU:1, one launch (start us, length us, event | category | flops | bytes accessed | tf_op | source)
XLA Modules:
  0.0 110.4 jit_solution(14875580439617051511)
XLA Ops:
  0.7 2.1 %shard_map.119 = (bf16[32,16,256]{2,1,0:T(8,128)(2,1)}, bf16[2,128,1024]{2,1,0:T(8,128)(2,1)}) custom-call(bf16[8,256]{1,0:T(8,128)(2,1)} %pk_ref.1, bf16[8,256]{1,0:T(8,128)(2,1)} %pv_ref.1, bf16[128,1024]{1,0:T(8,128)(2,1)} %rk_ref.1, bf16[128,1024]{1,0:T(8,128)(2,1)} %rv_ref.1), custom_call_target="tpu_custom_call" | custom-call | tf_op jit(solution)/shard_map/pallas_call | solution.py:215
  2.8 4.0 %collective-permute-start = (bf16[2,128,1024]{2,1,0:T(8,128)(2,1)}, bf16[2,128,1024]{2,1,0:T(8,128)(2,1)S(1)}, u32[]{:S(2)}, u32[]{:S(2)}) collective-permute-start(bf16[2,128,1024]{2,1,0:T(8,128)(2,1)} %get-tuple-element.33.kv_ref), channel_id=1, source_target_pairs={{0,1},{1,2},{2,3},{4,5},{5,6},{6,7},{8,9},{9,10},{10,11},{12,13},{... | collective-permute-start | bytes 1572872 | tf_op jit(solution)/shard_map/ppermute | solution.py:306
  6.7 11.2 %all-to-all-start = ((bf16[32,16,256]{2,1,0:T(8,128)(2,1)}), bf16[32,16,256]{2,1,0:T(8,128)(2,1)S(1)}, u32[]{:S(2)}, u32[]{:S(2)}) async-start(bf16[32,16,256]{2,1,0:T(8,128)(2,1)} %get-tuple-element.34), calls=%async_computation | async-start | bytes 524288 | tf_op jit(solution)/shard_map/all_to_all | solution.py:309
  18.0 4.4 %collective-permute-start.1 = (bf16[2,128,1024]{2,1,0:T(8,128)(2,1)}, bf16[2,128,1024]{2,1,0:T(8,128)(2,1)S(1)}, u32[]{:S(2)}, u32[]{:S(2)}) collective-permute-start(bf16[2,128,1024]{2,1,0:T(8,128)(2,1)} %get-tuple-element.33.kv_ref), channel_id=1, source_target_pairs={{0,2},{1,3},{4,6},{5,7},{8,10},{9,11},{12,14},{13,15},{16,18},{17,... | collective-permute-start | bytes 1572872 | tf_op jit(solution)/shard_map/ppermute | solution.py:307
  22.3 6.3 %all-to-all-done.mine_ref = bf16[32,16,256]{2,1,0:T(8,128)(2,1)S(1)} async-done(((bf16[32,16,256]{2,1,0:T(8,128)(2,1)}), bf16[32,16,256]{2,1,0:T(8,128)(2,1)S(1)}, u32[]{:S(2)}, u32[]{:S(2)}) %all-to-all-start) | async-done | bytes 262176 | tf_op jit(solution)/shard_map/all_to_all | solution.py:309
  28.6 3.2 %collective-permute-start.2 = (bf16[32,16,256]{2,1,0:T(8,128)(2,1)S(1)}, bf16[32,16,256]{2,1,0:T(8,128)(2,1)}, u32[]{:S(2)}, u32[]{:S(2)}) collective-permute-start(bf16[32,16,256]{2,1,0:T(8,128)(2,1)S(1)} %all-to-all-done.mine_ref), channel_id=1, source_target_pairs={{0,4},{4,0},{1,5},{5,1},{2,6},{6,2},{3,7},{7,3},{8,12},{12,8},{9,1... | collective-permute-start | bytes 786440 | tf_op jit(solution)/shard_map/ppermute | solution.py:311
  31.8 0.8 collective-permute-done.1.far_ref
  33.1 0.7 copy-done.8
  33.7 2.2 %shard_map.120.pr_ref = bf16[2,2,128,256]{3,2,1,0:T(8,128)(2,1)} custom-call(s32[1,2]{1,0:T(1,128)S(1)} %copy-done.8, s32[1]{0:T(128)} %bitcast.1.core_ref, bf16[32,16,256]{2,1,0:T(8,128)(2,1)S(1)} %all-to-all-done.mine_ref, bf16[32,16,256]{2,1,0:T(8,128)(2,1)} %collective-permute-done.2.other_ref, bf16[2,128,1024]{2,1,0:T(8,128)(2,1)S(1)} %collective-permute-done.near_ref, ...), custom_call_target="tpu_custom_call" | custom-call | tf_op jit(solution)/shard_map/pallas_call | solution.py:243
  36.0 1.2 %collective-permute-start.4 = (bf16[2,2,128,256]{3,2,1,0:T(8,128)(2,1)}, bf16[2,2,128,256]{3,2,1,0:T(8,128)(2,1)S(1)}, u32[]{:S(2)}, u32[]{:S(2)}) collective-permute-start(bf16[2,2,128,256]{3,2,1,0:T(8,128)(2,1)} %shard_map.120.pr_ref), channel_id=1, source_target_pairs={{0,1},{1,2},{2,3},{3,0},{4,5},{5,6},{6,7},{7,4},{8,9},{9,10},{10,1... | collective-permute-start | bytes 786440 | tf_op jit(solution)/shard_map/ppermute | solution.py:298
  37.2 1.9 %collective-permute-start.6 = (bf16[2,2,128,256]{3,2,1,0:T(8,128)(2,1)}, bf16[2,2,128,256]{3,2,1,0:T(8,128)(2,1)S(1)}, u32[]{:S(2)}, u32[]{:S(2)}) collective-permute-start(bf16[2,2,128,256]{3,2,1,0:T(8,128)(2,1)} %shard_map.120.pr_ref), channel_id=1, source_target_pairs={{0,2},{1,3},{2,0},{3,1},{4,6},{5,7},{6,4},{7,5},{8,10},{9,11},{10,... | collective-permute-start | bytes 786440 | tf_op jit(solution)/shard_map/ppermute | solution.py:298
  39.1 2.1 %collective-permute-start.3 = (bf16[2,2,128,256]{3,2,1,0:T(8,128)(2,1)}, bf16[2,2,128,256]{3,2,1,0:T(8,128)(2,1)S(1)}, u32[]{:S(2)}, u32[]{:S(2)}) collective-permute-start(bf16[2,2,128,256]{3,2,1,0:T(8,128)(2,1)} %shard_map.120.pr_ref), channel_id=1, source_target_pairs={{0,3},{1,0},{2,1},{3,2},{4,7},{5,4},{6,5},{7,6},{8,11},{9,8},{10,9... | collective-permute-start | bytes 786440 | tf_op jit(solution)/shard_map/ppermute | solution.py:298
  41.2 1.6 %copy-done.1 = bf16[128,8192]{1,0:T(8,128)(2,1)S(1)} copy-done((bf16[128,8192]{1,0:T(8,128)(2,1)S(1)}, bf16[128,8192]{1,0:T(8,128)(2,1)}, u32[]{:S(2)}) %copy-start.1) | copy-done | bytes 2097176
  42.8 1.0 copy-done.3
  43.8 1.0 copy-done.5
  44.9 1.0 copy-done.6
  45.9 6.7 %shard_map.121 = (bf16[128,8192]{1,0:T(8,128)(2,1)}, f32[2,128,1024]{2,1,0:T(8,128)S(1)}, bf16[2,128,1024]{2,1,0:T(8,128)(2,1)}, bf16[2,128,1024]{2,1,0:T(8,128)(2,1)}, bf16[2,2,128,256]{3,2,1,0:T(8,128)(2,1)S(1)}) custom-call(s32[1]{0:T(128)} %bitcast.sc_ref, s32[1,512]{1,0:T(1,128)S(1)} %copy-done.7, bf16[128,8192]{1,0:T(8,128)(2,1)S(1)} %copy-done, ...), custom_call_target="tpu_custom_call" | custom-call | flops 2684354560 | bytes 4194304 | tf_op jit(solution)/shard_map/pallas_call | solution.py:183
  52.6 6.0 %shard_map.122 = (bf16[128,8192]{1,0:T(8,128)(2,1)}, f32[2,128,1024]{2,1,0:T(8,128)S(1)}, bf16[2,128,1024]{2,1,0:T(8,128)(2,1)}, bf16[2,128,1024]{2,1,0:T(8,128)(2,1)}, bf16[2,2,128,256]{3,2,1,0:T(8,128)(2,1)S(1)}) custom-call(s32[1]{0:T(128)} %bitcast.sc_ref, ...), custom_call_target="tpu_custom_call", output_to_operand_aliasing={{0}: (8, {}), {1}: (9, {}), {2}: (10, {}), {3}: (11, {})} | custom-call | flops 2684354560 | bytes 4194304 | tf_op jit(solution)/shard_map/pallas_call | solution.py:183
  58.7 6.1 %shard_map.123 = (bf16[128,8192]{1,0:T(8,128)(2,1)}, f32[2,128,1024]{2,1,0:T(8,128)S(1)}, bf16[2,128,1024]{2,1,0:T(8,128)(2,1)}, bf16[2,128,1024]{2,1,0:T(8,128)(2,1)}, bf16[2,2,128,256]{3,2,1,0:T(8,128)(2,1)S(1)}) custom-call(s32[1]{0:T(128)} %bitcast.sc_ref, ...), custom_call_target="tpu_custom_call", output_to_operand_aliasing={{0}: (8, {}), {1}: (9, {}), {2}: (10, {}), {3}: (11, {})} | custom-call | flops 2684354560 | bytes 4194304 | tf_op jit(solution)/shard_map/pallas_call | solution.py:183
  64.8 1.1 %collective-permute-start.9 = (bf16[2,2,128,256]{3,2,1,0:T(8,128)(2,1)S(1)}, bf16[2,2,128,256]{3,2,1,0:T(8,128)(2,1)S(1)}, u32[]{:S(2)}, u32[]{:S(2)}) collective-permute-start(bf16[2,2,128,256]{3,2,1,0:T(8,128)(2,1)S(1)} %get-tuple-element.57), channel_id=1, source_target_pairs={{0,2},{1,3},{2,0},{3,1},{4,6},{5,7},{6,4},{7,5},{8,10},{9,11},{10,... | collective-permute-start | bytes 786440 | tf_op jit(solution)/shard_map/ppermute | solution.py:298
  65.9 6.1 %shard_map.124 = (bf16[128,8192]{1,0:T(8,128)(2,1)}, f32[2,128,1024]{2,1,0:T(8,128)S(1)}, bf16[2,128,1024]{2,1,0:T(8,128)(2,1)}, bf16[2,128,1024]{2,1,0:T(8,128)(2,1)}, bf16[2,2,128,256]{3,2,1,0:T(8,128)(2,1)S(1)}) custom-call(s32[1]{0:T(128)} %bitcast.sc_ref, ...), custom_call_target="tpu_custom_call", output_to_operand_aliasing={{0}: (8, {}), {1}: (9, {}), {2}: (10, {}), {3}: (11, {})} | custom-call | flops 2684354560 | bytes 4194304 | tf_op jit(solution)/shard_map/pallas_call | solution.py:183
  72.2 1.3 %collective-permute-start.7 = (bf16[2,128,1024]{2,1,0:T(8,128)(2,1)}, bf16[2,128,1024]{2,1,0:T(8,128)(2,1)S(1)}, u32[]{:S(2)}, u32[]{:S(2)}) collective-permute-start(bf16[2,128,1024]{2,1,0:T(8,128)(2,1)} %get-tuple-element.53), channel_id=1, source_target_pairs={{1,0},{2,1},{3,2},{5,4},{6,5},{7,6},{9,8},{10,9},{11,10},{13,12},{... | collective-permute-start | bytes 1572872 | tf_op jit(solution)/shard_map/ppermute | solution.py:326
  73.5 1.3 %collective-permute-start.8 = (bf16[2,128,1024]{2,1,0:T(8,128)(2,1)}, bf16[2,128,1024]{2,1,0:T(8,128)(2,1)S(1)}, u32[]{:S(2)}, u32[]{:S(2)}) collective-permute-start(bf16[2,128,1024]{2,1,0:T(8,128)(2,1)} %get-tuple-element.54), channel_id=1, source_target_pairs={{2,0},{3,1},{6,4},{7,5},{10,8},{11,9},{14,12},{15,13},{18,16},{19,... | collective-permute-start | bytes 1572872 | tf_op jit(solution)/shard_map/ppermute | solution.py:327
  74.8 3.6 %collective-permute-done.10.d_ref = bf16[2,2,128,256]{3,2,1,0:T(8,128)(2,1)S(1)} collective-permute-done((bf16[2,2,128,256]{3,2,1,0:T(8,128)(2,1)S(1)}, bf16[2,2,128,256]{3,2,1,0:T(8,128)(2,1)S(1)}, u32[]{:S(2)}, u32[]{:S(2)}) %collective-permute-start.10) | collective-permute-done | bytes 262176 | tf_op jit(solution)/shard_map/ppermute | solution.py:298
  78.5 0.8 shard_map.125
  79.3 7.1 %collective-permute-start.11 = (bf16[32,16,256]{2,1,0:T(8,128)(2,1)S(1)}, bf16[32,16,256]{2,1,0:T(8,128)(2,1)S(1)}, u32[]{:S(2)}, u32[]{:S(2)}) collective-permute-start(bf16[32,16,256]{2,1,0:T(8,128)(2,1)S(1)} %get-tuple-element.60), channel_id=1, source_target_pairs={{0,4},{4,0},{1,5},{5,1},{2,6},{6,2},{3,7},{7,3},{8,12},{12,8},{9,1... | collective-permute-start | bytes 786440 | tf_op jit(solution)/shard_map/ppermute | solution.py:330
  86.4 1.2 %collective-permute-done.11 = bf16[32,16,256]{2,1,0:T(8,128)(2,1)S(1)} collective-permute-done((bf16[32,16,256]{2,1,0:T(8,128)(2,1)S(1)}, bf16[32,16,256]{2,1,0:T(8,128)(2,1)S(1)}, u32[]{:S(2)}, u32[]{:S(2)}) %collective-permute-start.11) | collective-permute-done | bytes 262176 | tf_op jit(solution)/shard_map/ppermute | solution.py:330
  87.5 0.8 add_convert_fusion.1
  88.3 9.8 %all-to-all-start.1 = ((bf16[32,16,256]{2,1,0:T(8,128)(2,1)}), bf16[32,16,256]{2,1,0:T(8,128)(2,1)S(1)}, u32[]{:S(2)}, u32[]{:S(2)}) async-start(bf16[32,16,256]{2,1,0:T(8,128)(2,1)} %add_convert_fusion.1), calls=%async_computation.1 | async-start | bytes 524288 | tf_op jit(solution)/shard_map/all_to_all | solution.py:332
  98.4 0.8 slice_bitcast_fusion
  99.2 10.5 %all-to-all-done.1 = bf16[32,16,256]{2,1,0:T(8,128)(2,1)S(1)} async-done(((bf16[32,16,256]{2,1,0:T(8,128)(2,1)}), bf16[32,16,256]{2,1,0:T(8,128)(2,1)S(1)}, u32[]{:S(2)}, u32[]{:S(2)}) %all-to-all-start.1) | async-done | bytes 262176 | tf_op jit(solution)/shard_map/all_to_all | solution.py:332
  109.8 0.6 fusion
  (28 shorter events, 1.1 us)
Async XLA Ops:
  0.6 40.5 %copy-start.7 = (s32[1,512]{1,0:T(1,128)S(1)}, s32[1,512]{1,0:T(1,128)}, u32[]{:S(2)}) copy-start(s32[1,512]{1,0:T(1,128)} %seg_ref.7) | copy-start | bytes 6148
  0.6 40.5 %copy-start = (bf16[128,8192]{1,0:T(8,128)(2,1)S(1)}, bf16[128,8192]{1,0:T(8,128)(2,1)}, u32[]{:S(2)}) copy-start(bf16[128,8192]{1,0:T(8,128)(2,1)} %q_ref.7) | copy-start | bytes 6291460
  2.8 25.9 %collective-permute-start = (bf16[2,128,1024]{2,1,0:T(8,128)(2,1)}, bf16[2,128,1024]{2,1,0:T(8,128)(2,1)S(1)}, u32[]{:S(2)}, u32[]{:S(2)}) collective-permute-start(bf16[2,128,1024]{2,1,0:T(8,128)(2,1)} %get-tuple-element.33.kv_ref), channel_id=1, source_target_pairs={{0,1},{1,2},{2,3},{4,5},{5,6},{6,7},{8,9},{9,10},{10,11},{12,13},{... | collective-permute-start | bytes 1572872 | tf_op jit(solution)/shard_map/ppermute | solution.py:306
  6.7 21.9 %all-to-all-start = ((bf16[32,16,256]{2,1,0:T(8,128)(2,1)}), bf16[32,16,256]{2,1,0:T(8,128)(2,1)S(1)}, u32[]{:S(2)}, u32[]{:S(2)}) async-start(bf16[32,16,256]{2,1,0:T(8,128)(2,1)} %get-tuple-element.34), calls=%async_computation | async-start | bytes 524288 | tf_op jit(solution)/shard_map/all_to_all | solution.py:309
  18.0 14.6 %collective-permute-start.1 = (bf16[2,128,1024]{2,1,0:T(8,128)(2,1)}, bf16[2,128,1024]{2,1,0:T(8,128)(2,1)S(1)}, u32[]{:S(2)}, u32[]{:S(2)}) collective-permute-start(bf16[2,128,1024]{2,1,0:T(8,128)(2,1)} %get-tuple-element.33.kv_ref), channel_id=1, source_target_pairs={{0,2},{1,3},{4,6},{5,7},{8,10},{9,11},{12,14},{13,15},{16,18},{17,... | collective-permute-start | bytes 1572872 | tf_op jit(solution)/shard_map/ppermute | solution.py:307
  28.6 12.5 %copy-start.2 = (bf16[2,128,1024]{2,1,0:T(8,128)(2,1)}, bf16[2,128,1024]{2,1,0:T(8,128)(2,1)S(1)}, u32[]{:S(2)}) copy-start(bf16[2,128,1024]{2,1,0:T(8,128)(2,1)S(1)} %collective-permute-done.near_ref) | copy-start | bytes 1572868
  28.6 4.4 %collective-permute-start.2 = (bf16[32,16,256]{2,1,0:T(8,128)(2,1)S(1)}, bf16[32,16,256]{2,1,0:T(8,128)(2,1)}, u32[]{:S(2)}, u32[]{:S(2)}) collective-permute-start(bf16[32,16,256]{2,1,0:T(8,128)(2,1)S(1)} %all-to-all-done.mine_ref), channel_id=1, source_target_pairs={{0,4},{4,0},{1,5},{5,1},{2,6},{6,2},{3,7},{7,3},{8,12},{12,8},{9,1... | collective-permute-start | bytes 786440 | tf_op jit(solution)/shard_map/ppermute | solution.py:311
  32.6 8.6 %copy-start.4 = (bf16[2,128,1024]{2,1,0:T(8,128)(2,1)}, bf16[2,128,1024]{2,1,0:T(8,128)(2,1)S(1)}, u32[]{:S(2)}) copy-start(bf16[2,128,1024]{2,1,0:T(8,128)(2,1)S(1)} %collective-permute-done.1.far_ref) | copy-start | bytes 1572868
  33.1 0.7 copy-start.8
  36.0 16.6 %collective-permute-start.4 = (bf16[2,2,128,256]{3,2,1,0:T(8,128)(2,1)}, bf16[2,2,128,256]{3,2,1,0:T(8,128)(2,1)S(1)}, u32[]{:S(2)}, u32[]{:S(2)}) collective-permute-start(bf16[2,2,128,256]{3,2,1,0:T(8,128)(2,1)} %shard_map.120.pr_ref), channel_id=1, source_target_pairs={{0,1},{1,2},{2,3},{3,0},{4,5},{5,6},{6,7},{7,4},{8,9},{9,10},{10,1... | collective-permute-start | bytes 786440 | tf_op jit(solution)/shard_map/ppermute | solution.py:298
  37.2 21.5 %collective-permute-start.6 = (bf16[2,2,128,256]{3,2,1,0:T(8,128)(2,1)}, bf16[2,2,128,256]{3,2,1,0:T(8,128)(2,1)S(1)}, u32[]{:S(2)}, u32[]{:S(2)}) collective-permute-start(bf16[2,2,128,256]{3,2,1,0:T(8,128)(2,1)} %shard_map.120.pr_ref), channel_id=1, source_target_pairs={{0,2},{1,3},{2,0},{3,1},{4,6},{5,7},{6,4},{7,5},{8,10},{9,11},{10,... | collective-permute-start | bytes 786440 | tf_op jit(solution)/shard_map/ppermute | solution.py:298
  39.1 26.8 %collective-permute-start.3 = (bf16[2,2,128,256]{3,2,1,0:T(8,128)(2,1)}, bf16[2,2,128,256]{3,2,1,0:T(8,128)(2,1)S(1)}, u32[]{:S(2)}, u32[]{:S(2)}) collective-permute-start(bf16[2,2,128,256]{3,2,1,0:T(8,128)(2,1)} %shard_map.120.pr_ref), channel_id=1, source_target_pairs={{0,3},{1,0},{2,1},{3,2},{4,7},{5,4},{6,5},{7,6},{8,11},{9,8},{10,9... | collective-permute-start | bytes 786440 | tf_op jit(solution)/shard_map/ppermute | solution.py:298
  41.2 1.6 %copy-start.1 = (bf16[128,8192]{1,0:T(8,128)(2,1)S(1)}, bf16[128,8192]{1,0:T(8,128)(2,1)}, u32[]{:S(2)}) copy-start(bf16[128,8192]{1,0:T(8,128)(2,1)} %do_ref.7) | copy-start | bytes 6291460
  42.8 1.0 copy-start.3
  43.8 1.0 copy-start.5
  44.9 1.0 copy-start.6
  58.7 7.3 %collective-permute-start.5 = (bf16[2,2,128,256]{3,2,1,0:T(8,128)(2,1)S(1)}, bf16[2,2,128,256]{3,2,1,0:T(8,128)(2,1)S(1)}, u32[]{:S(2)}, u32[]{:S(2)}) collective-permute-start(bf16[2,2,128,256]{3,2,1,0:T(8,128)(2,1)S(1)} %get-tuple-element.41), channel_id=1, source_target_pairs={{0,3},{1,0},{2,1},{3,2},{4,7},{5,4},{6,5},{7,6},{8,11},{9,8},{10,9... | collective-permute-start | bytes 786440 | tf_op jit(solution)/shard_map/ppermute | solution.py:298
  64.8 10.1 %collective-permute-start.9 = (bf16[2,2,128,256]{3,2,1,0:T(8,128)(2,1)S(1)}, bf16[2,2,128,256]{3,2,1,0:T(8,128)(2,1)S(1)}, u32[]{:S(2)}, u32[]{:S(2)}) collective-permute-start(bf16[2,2,128,256]{3,2,1,0:T(8,128)(2,1)S(1)} %get-tuple-element.57), channel_id=1, source_target_pairs={{0,2},{1,3},{2,0},{3,1},{4,6},{5,7},{6,4},{7,5},{8,10},{9,11},{10,... | collective-permute-start | bytes 786440 | tf_op jit(solution)/shard_map/ppermute | solution.py:298
  65.9 12.5 %copy-start.9 = (s32[1,2]{1,0:T(1,128)S(1)}, s32[1,2]{1,0:T(1,128)}, u32[]{:S(2)}) copy-start(s32[1,2]{1,0:T(1,128)} %group_ref.3) | copy-start | bytes 28
  72.0 6.4 %collective-permute-start.10 = (bf16[2,2,128,256]{3,2,1,0:T(8,128)(2,1)S(1)}, bf16[2,2,128,256]{3,2,1,0:T(8,128)(2,1)S(1)}, u32[]{:S(2)}, u32[]{:S(2)}) collective-permute-start(bf16[2,2,128,256]{3,2,1,0:T(8,128)(2,1)S(1)} %get-tuple-element.58), channel_id=1, source_target_pairs={{0,1},{1,2},{2,3},{3,0},{4,5},{5,6},{6,7},{7,4},{8,9},{9,10},{10,1... | collective-permute-start | bytes 786440 | tf_op jit(solution)/shard_map/ppermute | solution.py:298
  72.2 25.9 %collective-permute-start.7 = (bf16[2,128,1024]{2,1,0:T(8,128)(2,1)}, bf16[2,128,1024]{2,1,0:T(8,128)(2,1)S(1)}, u32[]{:S(2)}, u32[]{:S(2)}) collective-permute-start(bf16[2,128,1024]{2,1,0:T(8,128)(2,1)} %get-tuple-element.53), channel_id=1, source_target_pairs={{1,0},{2,1},{3,2},{5,4},{6,5},{7,6},{9,8},{10,9},{11,10},{13,12},{... | collective-permute-start | bytes 1572872 | tf_op jit(solution)/shard_map/ppermute | solution.py:326
  73.5 24.6 %collective-permute-start.8 = (bf16[2,128,1024]{2,1,0:T(8,128)(2,1)}, bf16[2,128,1024]{2,1,0:T(8,128)(2,1)S(1)}, u32[]{:S(2)}, u32[]{:S(2)}) collective-permute-start(bf16[2,128,1024]{2,1,0:T(8,128)(2,1)} %get-tuple-element.54), channel_id=1, source_target_pairs={{2,0},{3,1},{6,4},{7,5},{10,8},{11,9},{14,12},{15,13},{18,16},{19,... | collective-permute-start | bytes 1572872 | tf_op jit(solution)/shard_map/ppermute | solution.py:327
  79.3 8.2 %collective-permute-start.11 = (bf16[32,16,256]{2,1,0:T(8,128)(2,1)S(1)}, bf16[32,16,256]{2,1,0:T(8,128)(2,1)S(1)}, u32[]{:S(2)}, u32[]{:S(2)}) collective-permute-start(bf16[32,16,256]{2,1,0:T(8,128)(2,1)S(1)} %get-tuple-element.60), channel_id=1, source_target_pairs={{0,4},{4,0},{1,5},{5,1},{2,6},{6,2},{3,7},{7,3},{8,12},{12,8},{9,1... | collective-permute-start | bytes 786440 | tf_op jit(solution)/shard_map/ppermute | solution.py:330
  88.3 21.4 %all-to-all-start.1 = ((bf16[32,16,256]{2,1,0:T(8,128)(2,1)}), bf16[32,16,256]{2,1,0:T(8,128)(2,1)S(1)}, u32[]{:S(2)}, u32[]{:S(2)}) async-start(bf16[32,16,256]{2,1,0:T(8,128)(2,1)} %add_convert_fusion.1), calls=%async_computation.1 | async-start | bytes 524288 | tf_op jit(solution)/shard_map/all_to_all | solution.py:332

commit v3 on v2

--- a/solution.py
+++ b/solution.py
@@ -63,7 +63,9 @@
     v_p=jnp.concatenate([pr_ref[0,1],pr_ref[1,1]],axis=1)
     ks=[k_p, far_ref[0],near_ref[0],kv_ref[0]]
     vs=[v_p, far_ref[1],near_ref[1],kv_ref[1]]
-    k_r_t=jnp.concatenate(ks[1:],axis=0).T
+    k_r=jnp.concatenate(ks[1:],axis=0)
+    v_r=jnp.concatenate(vs[1:],axis=0)
+    k_r_t=k_r.T
     k_p_t=jnp.concatenate([pr_ref[0,0],pr_ref[1,0]],axis=0).T
 
     st={}
@@ -75,17 +77,19 @@
     def two(x): return jnp.concatenate([x*first,x*second],axis=1)
     def s_chunk(p,c):
         q,_=load(p)
-        s=dot_nt(ks[c], two(q) if c==0 else q)
-        if c>0:
-            bc=bias[(c-1)*BLK:c*BLK]
-            s=s+jnp.concatenate([bc]*HEADS_STEP,axis=1)
-        ebuf[p%2][c*BLK:(c+1)*BLK]=s
-        m=fold(s,jnp.maximum)
-        st[p,"top"]=m if c==0 else jnp.maximum(st[p,"top"],m)
-        if c==3: st[p,"top"]=jnp.max(st[p,"top"],axis=0,keepdims=True)
+        if c==0:
+            s=dot_nt(k_p,two(q))
+            ebuf[p%2][:BLK]=s
+            st[p,"top"]=fold(s,jnp.maximum)
+        else:
+            s=dot_nt(k_r,q)+jnp.concatenate([bias[...]]*HEADS_STEP,axis=1)
+            ebuf[p%2][BLK:]=s
+            for j in range(3): st[p,"top"]=jnp.maximum(st[p,"top"],fold(s[j*BLK:(j+1)*BLK],jnp.maximum))
+        if c==1: st[p,"top"]=jnp.max(st[p,"top"],axis=0,keepdims=True)
     def g_chunk(p,c):
         _,do=load(p)
-        gbuf[p%2][c*BLK:(c+1)*BLK]=dot_nt(vs[c], two(do) if c==0 else do)
+        if c==0: gbuf[p%2][:BLK]=dot_nt(v_p,two(do))
+        else: gbuf[p%2][BLK:]=dot_nt(v_r,do)
     def pass2(p,c):
         sl=slice(c*BLK,(c+1)*BLK)
         e=jnp.exp2((ebuf[p%2][sl]-st[p,"top"])*LOG2_SCALE)
@@ -110,23 +114,24 @@
             dq_ref[:,cols(p,j)]=dq[j*BLK:(j+1)*BLK]
     def dk_part(p,c,kv):
         x=load(p)[kv]
-        src=(dsbuf,pbuf)[kv][p%2][c*BLK:(c+1)*BLK]
+        sr=slice(0,BLK) if c==0 else slice(BLK,4*BLK)
+        src=(dsbuf,pbuf)[kv][p%2][sr]
         r=dot_nn(src, two(x) if c==0 else x)
         acc=(dkacc,dvacc)[kv] if c>0 else (dkpacc,dvpacc)[kv]
-        sl=slice((c-1)*BLK,c*BLK) if c>0 else slice(0,BLK)
+        sl=slice(0,3*BLK) if c>0 else slice(0,BLK)
         if p==0: acc[sl]=r
         else: acc[sl]=acc[sl]+r
     def mk(p):
         l=[]
-        for c in range(4):
+        for c in range(2):
             l.append(lambda c=c: s_chunk(p,c))
-        for c in range(4):
+        for c in range(2):
             l.append(lambda c=c: g_chunk(p,c))
         return l
     def md(p):
         l=[lambda: dq_part(p)]
         for kv in range(2):
-            for c in range(4): l.append(lambda c=c,kv=kv: dk_part(p,c,kv))
+            for c in range(2): l.append(lambda c=c,kv=kv: dk_part(p,c,kv))
         return l
     def vp(p):
         return [lambda c=c: pass2(p,c) for c in range(4)]+[lambda c=c: pass3(p,c) for c in range(4)]
@@ -195,7 +200,7 @@
             + [pltpu.VMEM((BLK, 2 * HD), f32)] * 2,
         ),
         input_output_aliases=aliases,
-        compiler_params=pltpu.CompilerParams(vmem_limit_bytes=12 * 1024 * 1024),
+        compiler_params=pltpu.CompilerParams(vmem_limit_bytes=48 * 1024 * 1024),
         cost_estimate=pl.CostEstimate(
             flops=5 * 2 * 1024 * 512 * 128 * 2 * 2, bytes_accessed=4 << 20, transcendentals=1 << 20
         ),
@@ -324,9 +329,10 @@
         sent_back[d] = grad_prompts if d == 0 else shift(grad_prompts, "x", N_X, -d)
     out_q, own, grad_near, grad_far = carried
     back_near = lax.ppermute(grad_near, "x", [(1, 0), (2, 1), (3, 2)])
+
+    keep, give = spread(response_group, core, [sent_back[d] for d in range(N_X)])
+    give, grad_far = lax.optimization_barrier((give, grad_far))
     back_far = lax.ppermute(grad_far, "x", [(2, 0), (3, 1)])
-
-    keep, give = spread(response_group, core, [sent_back[d] for d in range(N_X)])
     got = lax.ppermute(give, "core", [(0, 1), (1, 0)])
     half = (keep + got.astype(f32)).astype(bf16)
     spread_out = lax.all_to_all(half, ("z", "y"), 0, 0)

time: 111 us -> 107 us (0.964)
  the two profiles are of different devices: /device:TPU:1 before, /device:TPU:4 now
where the time goes in v3:
time: 107 us
  starting transfers between devices  38.3 us (36%)
  waiting for transfers between devices  34.8 us (33%)
  Pallas kernels  29.9 us (28%)
  local copies, waits for them, and re-layouts  2.1 us (2%)
  other arithmetic  1.09 us (1%)
    pallas_call x4, Pallas kernels, attend(): pl.pallas_call(functools.partial(attention_kernel, slot), out_shape=out_s...  26.6 us
    all_to_all x1, waiting for transfers between devices, on_device(): spread_out = lax.all_to_all(half, ('z', 'y'), 0, 0)  12.1 us
    all_to_all x1, starting transfers between devices, on_device(): rows = lax.all_to_all(sent, ('z', 'y'), 0, 0)  11.5 us
    all_to_all x1, waiting for transfers between devices, on_device(): rows = lax.all_to_all(sent, ('z', 'y'), 0, 0)  11.3 us
    all_to_all x1, starting transfers between devices, on_device(): spread_out = lax.all_to_all(half, ('z', 'y'), 0, 0)  9.21 us
    ppermute x6, waiting for transfers between devices, shift(): return lax.ppermute(a, axis, [(i, (i + by) % size) for i in range(size)])  5.79 us
    ppermute x6, starting transfers between devices, shift(): return lax.ppermute(a, axis, [(i, (i + by) % size) for i in range(size)])  5.47 us
    ppermute x1, starting transfers between devices, on_device(): back_far = lax.ppermute(grad_far, 'x', [(2, 0), (3, 1)])  5.27 us
  transfers between devices with their start and end apart: 14, of which 6 were waited for; matrix products, arithmetic and copies ran while one was open for 2% of the time, Pallas kernels for 26%

profile of v3, /device:TPU:4, one launch (start us, length us, event | category | flops | bytes accessed | tf_op | source)
XLA Modules:
  0.0 107.0 jit_solution(12675349292276206487)
XLA Ops:
  0.6 2.0 %shard_map.119 = (bf16[32,16,256]{2,1,0:T(8,128)(2,1)}, bf16[2,128,1024]{2,1,0:T(8,128)(2,1)}) custom-call(bf16[8,256]{1,0:T(8,128)(2,1)} %pk_ref.1, bf16[8,256]{1,0:T(8,128)(2,1)} %pv_ref.1, bf16[128,1024]{1,0:T(8,128)(2,1)} %rk_ref.1, bf16[128,1024]{1,0:T(8,128)(2,1)} %rv_ref.1), custom_call_target="tpu_custom_call" | custom-call | tf_op jit(solution)/shard_map/pallas_call | solution.py:220
  2.6 3.2 %collective-permute-start = (bf16[2,128,1024]{2,1,0:T(8,128)(2,1)}, bf16[2,128,1024]{2,1,0:T(8,128)(2,1)S(1)}, u32[]{:S(2)}, u32[]{:S(2)}) collective-permute-start(bf16[2,128,1024]{2,1,0:T(8,128)(2,1)} %get-tuple-element.35.kv_ref), channel_id=1, source_target_pairs={{0,1},{1,2},{2,3},{4,5},{5,6},{6,7},{8,9},{9,10},{10,11},{12,13},{... | collective-permute-start | bytes 1572872 | tf_op jit(solution)/shard_map/ppermute | solution.py:311
  5.9 11.5 %all-to-all-start = ((bf16[32,16,256]{2,1,0:T(8,128)(2,1)}), bf16[32,16,256]{2,1,0:T(8,128)(2,1)S(1)}, u32[]{:S(2)}, u32[]{:S(2)}) async-start(bf16[32,16,256]{2,1,0:T(8,128)(2,1)} %get-tuple-element.36), calls=%async_computation | async-start | bytes 524288 | tf_op jit(solution)/shard_map/all_to_all | solution.py:314
  17.4 1.3 %collective-permute-start.1 = (bf16[2,128,1024]{2,1,0:T(8,128)(2,1)}, bf16[2,128,1024]{2,1,0:T(8,128)(2,1)S(1)}, u32[]{:S(2)}, u32[]{:S(2)}) collective-permute-start(bf16[2,128,1024]{2,1,0:T(8,128)(2,1)} %get-tuple-element.35.kv_ref), channel_id=1, source_target_pairs={{0,2},{1,3},{4,6},{5,7},{8,10},{9,11},{12,14},{13,15},{16,18},{17,... | collective-permute-start | bytes 1572872 | tf_op jit(solution)/shard_map/ppermute | solution.py:312
  18.7 11.3 %all-to-all-done.mine_ref = bf16[32,16,256]{2,1,0:T(8,128)(2,1)S(1)} async-done(((bf16[32,16,256]{2,1,0:T(8,128)(2,1)}), bf16[32,16,256]{2,1,0:T(8,128)(2,1)S(1)}, u32[]{:S(2)}, u32[]{:S(2)}) %all-to-all-start) | async-done | bytes 262176 | tf_op jit(solution)/shard_map/all_to_all | solution.py:314
  29.9 0.0 collective-permute-start.2
  29.9 4.1 %collective-permute-done.1.far_ref = bf16[2,128,1024]{2,1,0:T(8,128)(2,1)S(1)} collective-permute-done((bf16[2,128,1024]{2,1,0:T(8,128)(2,1)}, bf16[2,128,1024]{2,1,0:T(8,128)(2,1)S(1)}, u32[]{:S(2)}, u32[]{:S(2)}) %collective-permute-start.1) | collective-permute-done | bytes 524320 | tf_op jit(solution)/shard_map/ppermute | solution.py:312
  34.1 0.0 collective-permute-done.2.other_ref
  34.1 0.7 copy-done.2
  34.7 0.6 shard_map.120.pr_ref
  35.3 0.1 collective-permute-start.4
  35.4 0.1 collective-permute-start.6
  35.5 2.2 %collective-permute-start.3 = (bf16[2,2,128,256]{3,2,1,0:T(8,128)(2,1)S(1)}, bf16[2,2,128,256]{3,2,1,0:T(8,128)(2,1)S(1)}, u32[]{:S(2)}, u32[]{:S(2)}) collective-permute-start(bf16[2,2,128,256]{3,2,1,0:T(8,128)(2,1)S(1)} %shard_map.120.pr_ref), channel_id=1, source_target_pairs={{0,3},{1,0},{2,1},{3,2},{4,7},{5,4},{6,5},{7,6},{8,11},{9,8},{10,9... | collective-permute-start | bytes 786440 | tf_op jit(solution)/shard_map/ppermute | solution.py:303
  37.7 6.6 %shard_map.121 = (bf16[128,8192]{1,0:T(8,128)(2,1)}, f32[2,128,1024]{2,1,0:T(8,128)S(1)}, bf16[2,128,1024]{2,1,0:T(8,128)(2,1)S(1)}, bf16[2,128,1024]{2,1,0:T(8,128)(2,1)}, bf16[2,2,128,256]{3,2,1,0:T(8,128)(2,1)S(1)}) custom-call(s32[1]{0:T(128)} %bitcast.sc_ref, s32[1,512]{1,0:T(1,128)S(1)} %copy-done.1, bf16[128,8192]{1,0:T(8,128)(2,1)} %q_ref.7, ...), custom_call_target="tpu_custom_call" | custom-call | flops 2684354560 | bytes 4194304 | tf_op jit(solution)/shard_map/pallas_call | solution.py:188
  44.3 3.3 %collective-permute-done.4.pr_ref = bf16[2,2,128,256]{3,2,1,0:T(8,128)(2,1)} collective-permute-done((bf16[2,2,128,256]{3,2,1,0:T(8,128)(2,1)S(1)}, bf16[2,2,128,256]{3,2,1,0:T(8,128)(2,1)}, u32[]{:S(2)}, u32[]{:S(2)}) %collective-permute-start.4) | collective-permute-done | bytes 262176 | tf_op jit(solution)/shard_map/ppermute | solution.py:303
  47.7 6.6 %shard_map.122 = (bf16[128,8192]{1,0:T(8,128)(2,1)}, f32[2,128,1024]{2,1,0:T(8,128)S(1)}, bf16[2,128,1024]{2,1,0:T(8,128)(2,1)S(1)}, bf16[2,128,1024]{2,1,0:T(8,128)(2,1)}, bf16[2,2,128,256]{3,2,1,0:T(8,128)(2,1)S(1)}) custom-call(s32[1]{0:T(128)} %bitcast.sc_ref, ...), custom_call_target="tpu_custom_call", output_to_operand_aliasing={{0}: (8, {}), {1}: (9, {}), {2}: (10, {}), {3}: (11, {})} | custom-call | flops 2684354560 | bytes 4194304 | tf_op jit(solution)/shard_map/pallas_call | solution.py:188
  54.3 6.7 %shard_map.123 = (bf16[128,8192]{1,0:T(8,128)(2,1)}, f32[2,128,1024]{2,1,0:T(8,128)S(1)}, bf16[2,128,1024]{2,1,0:T(8,128)(2,1)S(1)}, bf16[2,128,1024]{2,1,0:T(8,128)(2,1)}, bf16[2,2,128,256]{3,2,1,0:T(8,128)(2,1)S(1)}) custom-call(s32[1]{0:T(128)} %bitcast.sc_ref, ...), custom_call_target="tpu_custom_call", output_to_operand_aliasing={{0}: (8, {}), {1}: (9, {}), {2}: (10, {}), {3}: (11, {})} | custom-call | flops 2684354560 | bytes 4194304 | tf_op jit(solution)/shard_map/pallas_call | solution.py:188
  61.0 0.6 collective-permute-start.8
  61.6 6.6 %shard_map.124 = (bf16[128,8192]{1,0:T(8,128)(2,1)}, f32[2,128,1024]{2,1,0:T(8,128)S(1)}, bf16[2,128,1024]{2,1,0:T(8,128)(2,1)S(1)}, bf16[2,128,1024]{2,1,0:T(8,128)(2,1)}, bf16[2,2,128,256]{3,2,1,0:T(8,128)(2,1)S(1)}) custom-call(s32[1]{0:T(128)} %bitcast.sc_ref, ...), custom_call_target="tpu_custom_call", output_to_operand_aliasing={{0}: (8, {}), {1}: (9, {}), {2}: (10, {}), {3}: (11, {})} | custom-call | flops 2684354560 | bytes 4194304 | tf_op jit(solution)/shard_map/pallas_call | solution.py:188
  68.2 2.5 %collective-permute-start.9 = (bf16[2,2,128,256]{3,2,1,0:T(8,128)(2,1)S(1)}, bf16[2,2,128,256]{3,2,1,0:T(8,128)(2,1)S(1)}, u32[]{:S(2)}, u32[]{:S(2)}) collective-permute-start(bf16[2,2,128,256]{3,2,1,0:T(8,128)(2,1)S(1)} %get-tuple-element.59), channel_id=1, source_target_pairs={{0,1},{1,2},{2,3},{3,0},{4,5},{5,6},{6,7},{7,4},{8,9},{9,10},{10,1... | collective-permute-start | bytes 786440 | tf_op jit(solution)/shard_map/ppermute | solution.py:303
  70.8 2.2 %collective-permute-start.7 = (bf16[2,128,1024]{2,1,0:T(8,128)(2,1)S(1)}, bf16[2,128,1024]{2,1,0:T(8,128)(2,1)S(1)}, u32[]{:S(2)}, u32[]{:S(2)}) collective-permute-start(bf16[2,128,1024]{2,1,0:T(8,128)(2,1)S(1)} %get-tuple-element.55), channel_id=1, source_target_pairs={{1,0},{2,1},{3,2},{5,4},{6,5},{7,6},{9,8},{10,9},{11,10},{13,12},{... | collective-permute-start | bytes 1572872 | tf_op jit(solution)/shard_map/ppermute | solution.py:331
  73.0 2.4 %collective-permute-done.9.d_ref = bf16[2,2,128,256]{3,2,1,0:T(8,128)(2,1)S(1)} collective-permute-done((bf16[2,2,128,256]{3,2,1,0:T(8,128)(2,1)S(1)}, bf16[2,2,128,256]{3,2,1,0:T(8,128)(2,1)S(1)}, u32[]{:S(2)}, u32[]{:S(2)}) %collective-permute-start.9) | collective-permute-done | bytes 262176 | tf_op jit(solution)/shard_map/ppermute | solution.py:303
  75.4 0.8 shard_map.125
  76.2 5.3 %collective-permute-start.10 = (bf16[2,128,1024]{2,1,0:T(8,128)(2,1)}, bf16[2,128,1024]{2,1,0:T(8,128)(2,1)S(1)}, u32[]{:S(2)}, u32[]{:S(2)}) collective-permute-start(bf16[2,128,1024]{2,1,0:T(8,128)(2,1)} %get-tuple-element.62), channel_id=1, source_target_pairs={{2,0},{3,1},{6,4},{7,5},{10,8},{11,9},{14,12},{15,13},{18,16},{19,... | collective-permute-start | bytes 1572872 | tf_op jit(solution)/shard_map/ppermute | solution.py:335
  81.5 0.1 collective-permute-start.11
  81.6 1.5 %collective-permute-done.11 = bf16[32,16,256]{2,1,0:T(8,128)(2,1)S(1)} collective-permute-done((bf16[32,16,256]{2,1,0:T(8,128)(2,1)S(1)}, bf16[32,16,256]{2,1,0:T(8,128)(2,1)S(1)}, u32[]{:S(2)}, u32[]{:S(2)}) %collective-permute-start.11) | collective-permute-done | bytes 262176 | tf_op jit(solution)/shard_map/ppermute | solution.py:336
  83.1 0.8 add_convert_fusion.1
  83.9 9.2 %all-to-all-start.1 = ((bf16[32,16,256]{2,1,0:T(8,128)(2,1)}), bf16[32,16,256]{2,1,0:T(8,128)(2,1)S(1)}, u32[]{:S(2)}, u32[]{:S(2)}) async-start(bf16[32,16,256]{2,1,0:T(8,128)(2,1)} %add_convert_fusion.1), calls=%async_computation.1 | async-start | bytes 524288 | tf_op jit(solution)/shard_map/all_to_all | solution.py:338
  93.2 0.3 add_convert_fusion
  93.4 0.8 slice_bitcast_fusion
  94.3 12.1 %all-to-all-done.1 = bf16[32,16,256]{2,1,0:T(8,128)(2,1)S(1)} async-done(((bf16[32,16,256]{2,1,0:T(8,128)(2,1)}), bf16[32,16,256]{2,1,0:T(8,128)(2,1)S(1)}, u32[]{:S(2)}, u32[]{:S(2)}) %all-to-all-start.1) | async-done | bytes 262176 | tf_op jit(solution)/shard_map/all_to_all | solution.py:338
  106.4 0.6 fusion
  (16 shorter events, 0.1 us)
Async XLA Ops:
  0.6 37.1 %copy-start.1 = (s32[1,512]{1,0:T(1,128)S(1)}, s32[1,512]{1,0:T(1,128)}, u32[]{:S(2)}) copy-start(s32[1,512]{1,0:T(1,128)} %seg_ref.7) | copy-start | bytes 6148
  2.6 35.1 %copy-start = (bf16[2,128,1024]{2,1,0:T(8,128)(2,1)S(1)}, bf16[2,128,1024]{2,1,0:T(8,128)(2,1)}, u32[]{:S(2)}) copy-start(bf16[2,128,1024]{2,1,0:T(8,128)(2,1)} %get-tuple-element.35.kv_ref) | copy-start | bytes 1572868
  2.6 27.3 %collective-permute-start = (bf16[2,128,1024]{2,1,0:T(8,128)(2,1)}, bf16[2,128,1024]{2,1,0:T(8,128)(2,1)S(1)}, u32[]{:S(2)}, u32[]{:S(2)}) collective-permute-start(bf16[2,128,1024]{2,1,0:T(8,128)(2,1)} %get-tuple-element.35.kv_ref), channel_id=1, source_target_pairs={{0,1},{1,2},{2,3},{4,5},{5,6},{6,7},{8,9},{9,10},{10,11},{12,13},{... | collective-permute-start | bytes 1572872 | tf_op jit(solution)/shard_map/ppermute | solution.py:311
  5.9 24.1 %all-to-all-start = ((bf16[32,16,256]{2,1,0:T(8,128)(2,1)}), bf16[32,16,256]{2,1,0:T(8,128)(2,1)S(1)}, u32[]{:S(2)}, u32[]{:S(2)}) async-start(bf16[32,16,256]{2,1,0:T(8,128)(2,1)} %get-tuple-element.36), calls=%async_computation | async-start | bytes 524288 | tf_op jit(solution)/shard_map/all_to_all | solution.py:314
  17.4 16.7 %collective-permute-start.1 = (bf16[2,128,1024]{2,1,0:T(8,128)(2,1)}, bf16[2,128,1024]{2,1,0:T(8,128)(2,1)S(1)}, u32[]{:S(2)}, u32[]{:S(2)}) collective-permute-start(bf16[2,128,1024]{2,1,0:T(8,128)(2,1)} %get-tuple-element.35.kv_ref), channel_id=1, source_target_pairs={{0,2},{1,3},{4,6},{5,7},{8,10},{9,11},{12,14},{13,15},{16,18},{17,... | collective-permute-start | bytes 1572872 | tf_op jit(solution)/shard_map/ppermute | solution.py:312
  29.9 4.1 %collective-permute-start.2 = (bf16[32,16,256]{2,1,0:T(8,128)(2,1)S(1)}, bf16[32,16,256]{2,1,0:T(8,128)(2,1)S(1)}, u32[]{:S(2)}, u32[]{:S(2)}) collective-permute-start(bf16[32,16,256]{2,1,0:T(8,128)(2,1)S(1)} %all-to-all-done.mine_ref), channel_id=1, source_target_pairs={{0,4},{4,0},{1,5},{5,1},{2,6},{6,2},{3,7},{7,3},{8,12},{12,8},{9,1... | collective-permute-start | bytes 786440 | tf_op jit(solution)/shard_map/ppermute | solution.py:316
  34.1 0.7 copy-start.2
  35.3 12.4 %collective-permute-start.4 = (bf16[2,2,128,256]{3,2,1,0:T(8,128)(2,1)S(1)}, bf16[2,2,128,256]{3,2,1,0:T(8,128)(2,1)}, u32[]{:S(2)}, u32[]{:S(2)}) collective-permute-start(bf16[2,2,128,256]{3,2,1,0:T(8,128)(2,1)S(1)} %shard_map.120.pr_ref), channel_id=1, source_target_pairs={{0,1},{1,2},{2,3},{3,0},{4,5},{5,6},{6,7},{7,4},{8,9},{9,10},{10,1... | collective-permute-start | bytes 786440 | tf_op jit(solution)/shard_map/ppermute | solution.py:303
  35.4 18.9 %collective-permute-start.6 = (bf16[2,2,128,256]{3,2,1,0:T(8,128)(2,1)S(1)}, bf16[2,2,128,256]{3,2,1,0:T(8,128)(2,1)S(1)}, u32[]{:S(2)}, u32[]{:S(2)}) collective-permute-start(bf16[2,2,128,256]{3,2,1,0:T(8,128)(2,1)S(1)} %shard_map.120.pr_ref), channel_id=1, source_target_pairs={{0,2},{1,3},{2,0},{3,1},{4,6},{5,7},{6,4},{7,5},{8,10},{9,11},{10,... | collective-permute-start | bytes 786440 | tf_op jit(solution)/shard_map/ppermute | solution.py:303
  35.5 26.1 %collective-permute-start.3 = (bf16[2,2,128,256]{3,2,1,0:T(8,128)(2,1)S(1)}, bf16[2,2,128,256]{3,2,1,0:T(8,128)(2,1)S(1)}, u32[]{:S(2)}, u32[]{:S(2)}) collective-permute-start(bf16[2,2,128,256]{3,2,1,0:T(8,128)(2,1)S(1)} %shard_map.120.pr_ref), channel_id=1, source_target_pairs={{0,3},{1,0},{2,1},{3,2},{4,7},{5,4},{6,5},{7,6},{8,11},{9,8},{10,9... | collective-permute-start | bytes 786440 | tf_op jit(solution)/shard_map/ppermute | solution.py:303
  54.3 7.3 %collective-permute-start.5 = (bf16[2,2,128,256]{3,2,1,0:T(8,128)(2,1)S(1)}, bf16[2,2,128,256]{3,2,1,0:T(8,128)(2,1)S(1)}, u32[]{:S(2)}, u32[]{:S(2)}) collective-permute-start(bf16[2,2,128,256]{3,2,1,0:T(8,128)(2,1)S(1)} %get-tuple-element.43), channel_id=1, source_target_pairs={{0,3},{1,0},{2,1},{3,2},{4,7},{5,4},{6,5},{7,6},{8,11},{9,8},{10,9... | collective-permute-start | bytes 786440 | tf_op jit(solution)/shard_map/ppermute | solution.py:303
  61.0 12.0 %collective-permute-start.8 = (bf16[2,2,128,256]{3,2,1,0:T(8,128)(2,1)S(1)}, bf16[2,2,128,256]{3,2,1,0:T(8,128)(2,1)S(1)}, u32[]{:S(2)}, u32[]{:S(2)}) collective-permute-start(bf16[2,2,128,256]{3,2,1,0:T(8,128)(2,1)S(1)} %get-tuple-element.58), channel_id=1, source_target_pairs={{0,2},{1,3},{2,0},{3,1},{4,6},{5,7},{6,4},{7,5},{8,10},{9,11},{10,... | collective-permute-start | bytes 786440 | tf_op jit(solution)/shard_map/ppermute | solution.py:303
  61.6 13.8 %copy-start.3 = (s32[1,2]{1,0:T(1,128)S(1)}, s32[1,2]{1,0:T(1,128)}, u32[]{:S(2)}) copy-start(s32[1,2]{1,0:T(1,128)} %group_ref.3) | copy-start | bytes 28
  68.2 7.2 %collective-permute-start.9 = (bf16[2,2,128,256]{3,2,1,0:T(8,128)(2,1)S(1)}, bf16[2,2,128,256]{3,2,1,0:T(8,128)(2,1)S(1)}, u32[]{:S(2)}, u32[]{:S(2)}) collective-permute-start(bf16[2,2,128,256]{3,2,1,0:T(8,128)(2,1)S(1)} %get-tuple-element.59), channel_id=1, source_target_pairs={{0,1},{1,2},{2,3},{3,0},{4,5},{5,6},{6,7},{7,4},{8,9},{9,10},{10,1... | collective-permute-start | bytes 786440 | tf_op jit(solution)/shard_map/ppermute | solution.py:303
  70.8 22.4 %collective-permute-start.7 = (bf16[2,128,1024]{2,1,0:T(8,128)(2,1)S(1)}, bf16[2,128,1024]{2,1,0:T(8,128)(2,1)S(1)}, u32[]{:S(2)}, u32[]{:S(2)}) collective-permute-start(bf16[2,128,1024]{2,1,0:T(8,128)(2,1)S(1)} %get-tuple-element.55), channel_id=1, source_target_pairs={{1,0},{2,1},{3,2},{5,4},{6,5},{7,6},{9,8},{10,9},{11,10},{13,12},{... | collective-permute-start | bytes 1572872 | tf_op jit(solution)/shard_map/ppermute | solution.py:331
  76.2 16.9 %collective-permute-start.10 = (bf16[2,128,1024]{2,1,0:T(8,128)(2,1)}, bf16[2,128,1024]{2,1,0:T(8,128)(2,1)S(1)}, u32[]{:S(2)}, u32[]{:S(2)}) collective-permute-start(bf16[2,128,1024]{2,1,0:T(8,128)(2,1)} %get-tuple-element.62), channel_id=1, source_target_pairs={{2,0},{3,1},{6,4},{7,5},{10,8},{11,9},{14,12},{15,13},{18,16},{19,... | collective-permute-start | bytes 1572872 | tf_op jit(solution)/shard_map/ppermute | solution.py:335
  81.5 1.6 %collective-permute-start.11 = (bf16[32,16,256]{2,1,0:T(8,128)(2,1)S(1)}, bf16[32,16,256]{2,1,0:T(8,128)(2,1)S(1)}, u32[]{:S(2)}, u32[]{:S(2)}) collective-permute-start(bf16[32,16,256]{2,1,0:T(8,128)(2,1)S(1)} %get-tuple-element.64), channel_id=1, source_target_pairs={{0,4},{4,0},{1,5},{5,1},{2,6},{6,2},{3,7},{7,3},{8,12},{12,8},{9,1... | collective-permute-start | bytes 786440 | tf_op jit(solution)/shard_map/ppermute | solution.py:336
  83.9 22.5 %all-to-all-start.1 = ((bf16[32,16,256]{2,1,0:T(8,128)(2,1)}), bf16[32,16,256]{2,1,0:T(8,128)(2,1)S(1)}, u32[]{:S(2)}, u32[]{:S(2)}) async-start(bf16[32,16,256]{2,1,0:T(8,128)(2,1)} %add_convert_fusion.1), calls=%async_computation.1 | async-start | bytes 524288 | tf_op jit(solution)/shard_map/all_to_all | solution.py:338

commit v4 on v3

--- a/solution.py
+++ b/solution.py
@@ -155,9 +155,9 @@
         dpr_ref[0,j]=(pp[:,:HD]*sc_).astype(bf16)
         dpr_ref[1,j]=(pp[:,HD:]*sc_).astype(bf16)
 
-def attend(slot, place, seg, q, do, kv, near, far, prompts, carried):
+def attend(slot, place, seg, q, do, kv, near, far, prompts, carried, start=0, count=2):
     def head_of(i, sc):
-        return 2 * lax.rem(sc[0] + (N_X - slot), N_X) + i
+        return 2 * lax.rem(sc[0] + (N_X - slot), N_X) + (i + start)
 
     def at_head(i, sc):
         return (0, head_of(i, sc))
@@ -168,7 +168,7 @@
     wide_spec = pl.BlockSpec((BLK, HEAD_COLS), at_head)
     one_spec = pl.BlockSpec((BLK, HD), at_head)
     pair_spec = pl.BlockSpec((2, BLK, HD), pair_at_head)
-    prompt_spec = pl.BlockSpec((2, 2, BLK, HD), lambda i, sc: (0, 0, 0, i))
+    prompt_spec = pl.BlockSpec((2, 2, BLK, HD), lambda i, sc: (0, 0, 0, i + start))
     seg_spec = pl.BlockSpec((1, 512), lambda i, sc: (0, 0))
     out_shape = (
         jax.ShapeDtypeStruct((BLK, KV_HEADS * HEAD_COLS), bf16),
@@ -190,7 +190,7 @@
         out_shape=out_shape,
         grid_spec=pltpu.PrefetchScalarGridSpec(
             num_scalar_prefetch=1,
-            grid=(2,),
+            grid=(count,),
             in_specs=in_specs,
             out_specs=(wide_spec, pair_spec, pair_spec, pair_spec, prompt_spec),
             scratch_shapes=[pltpu.VMEM((3 * BLK, BLK), f32)]
@@ -319,14 +319,15 @@
 
     carried = None
     sent_back = {}
-    for d in (0, 1, 2, 3):
+    inputs = (place, segment_ids, q, do, kv, near, far)
+    *carried, own_grad = attend(0, *inputs, slots[0], None, 0, 1)
+    for d in (1, 2, 3):
         prompts = slots[d]
         if d == 3:
             prompts, sent_back[1] = lax.optimization_barrier((prompts, sent_back[1]))
-        *carried, grad_prompts = attend(
-            d, place, segment_ids, q, do, kv, near, far, prompts, carried
-        )
-        sent_back[d] = grad_prompts if d == 0 else shift(grad_prompts, "x", N_X, -d)
+        *carried, grad_prompts = attend(d, *inputs, prompts, carried)
+        sent_back[d] = shift(grad_prompts, "x", N_X, -d)
+    *carried, sent_back[0] = attend(0, *inputs, slots[0], [*carried, own_grad], 1, 1)
     out_q, own, grad_near, grad_far = carried
     back_near = lax.ppermute(grad_near, "x", [(1, 0), (2, 1), (3, 2)])
 

time: 107 us -> 114 us (1.065)
  starting transfers between devices: 38.3 us -> 41.9 us
  Pallas kernels: 29.9 us -> 31.1 us
    ppermute x1, starting transfers between devices: 5.27 us -> 10.1 us  [on_device(): back_far = lax.ppermute(grad_far, 'x', [(2, 0), (3, 1)])]
    ppermute x6, starting transfers between devices: 5.47 us -> 3.25 us  [shift(): return lax.ppermute(a, axis, [(i, (i + by) % size) for i in range(size)])]
    ppermute x6, waiting for transfers between devices: 5.79 us -> 7.19 us  [shift(): return lax.ppermute(a, axis, [(i, (i + by) % size) for i in range(size)])]
    pallas_call x4 -> x5, Pallas kernels: 26.6 us -> 27.8 us  [attend(): pl.pallas_call(functools.partial(attention_kernel, slot), out_shape=out_s...]
    ppermute x1, starting transfers between devices: 2.21 us -> 3.35 us  [on_device(): back_near = lax.ppermute(grad_near, 'x', [(1, 0), (2, 1), (3, 2)])]
  transfers between devices with their start and end apart: 14 -> 14, of which waited for: 6 -> 6; matrix products, arithmetic and copies ran while one was open for 2% -> 3% of each run, Pallas kernels for 26% -> 25%
where the time goes in v4:
time: 114 us; the launch traced here: 113 us
  starting transfers between devices  41.9 us (37%)
  waiting for transfers between devices  35.2 us (31%)
  Pallas kernels  31.1 us (27%)
  other arithmetic  2.14 us (2%)
  local copies, waits for them, and re-layouts  2.1 us (2%)
    pallas_call x5, Pallas kernels, attend(): pl.pallas_call(functools.partial(attention_kernel, slot), out_shape=out_s...  27.8 us
    all_to_all x1, starting transfers between devices, on_device(): rows = lax.all_to_all(sent, ('z', 'y'), 0, 0)  11.5 us
    all_to_all x1, waiting for transfers between devices, on_device(): rows = lax.all_to_all(sent, ('z', 'y'), 0, 0)  11.3 us
    all_to_all x1, waiting for transfers between devices, on_device(): spread_out = lax.all_to_all(half, ('z', 'y'), 0, 0)  11.1 us
    ppermute x1, starting transfers between devices, on_device(): back_far = lax.ppermute(grad_far, 'x', [(2, 0), (3, 1)])  10.1 us
    all_to_all x1, starting transfers between devices, on_device(): spread_out = lax.all_to_all(half, ('z', 'y'), 0, 0)  9.22 us
    ppermute x6, waiting for transfers between devices, shift(): return lax.ppermute(a, axis, [(i, (i + by) % size) for i in range(size)])  7.19 us
    ppermute x1, waiting for transfers between devices, on_device(): far = lax.ppermute(kv, 'x', [(0, 2), (1, 3)])  4.12 us
  transfers between devices with their start and end apart: 14, of which 6 were waited for; matrix products, arithmetic and copies ran while one was open for 3% of the time, Pallas kernels for 25%

profile of v4, /device:TPU:4, one launch (start us, length us, event | category | flops | bytes accessed | tf_op | source)
XLA Modules:
  0.0 113.3 jit_solution(11475916603551385598)
XLA Ops:
  0.6 2.0 %shard_map.119 = (bf16[32,16,256]{2,1,0:T(8,128)(2,1)}, bf16[2,128,1024]{2,1,0:T(8,128)(2,1)}) custom-call(bf16[8,256]{1,0:T(8,128)(2,1)} %pk_ref.1, bf16[8,256]{1,0:T(8,128)(2,1)} %pv_ref.1, bf16[128,1024]{1,0:T(8,128)(2,1)} %rk_ref.1, bf16[128,1024]{1,0:T(8,128)(2,1)} %rv_ref.1), custom_call_target="tpu_custom_call" | custom-call | tf_op jit(solution)/shard_map/pallas_call | solution.py:220
  2.6 3.2 %collective-permute-start = (bf16[2,128,1024]{2,1,0:T(8,128)(2,1)}, bf16[2,128,1024]{2,1,0:T(8,128)(2,1)S(1)}, u32[]{:S(2)}, u32[]{:S(2)}) collective-permute-start(bf16[2,128,1024]{2,1,0:T(8,128)(2,1)} %get-tuple-element.40.kv_ref), channel_id=1, source_target_pairs={{0,1},{1,2},{2,3},{4,5},{5,6},{6,7},{8,9},{9,10},{10,11},{12,13},{... | collective-permute-start | bytes 1572872 | tf_op jit(solution)/shard_map/ppermute | solution.py:311
  5.9 11.5 %all-to-all-start = ((bf16[32,16,256]{2,1,0:T(8,128)(2,1)}), bf16[32,16,256]{2,1,0:T(8,128)(2,1)S(1)}, u32[]{:S(2)}, u32[]{:S(2)}) async-start(bf16[32,16,256]{2,1,0:T(8,128)(2,1)} %get-tuple-element.41), calls=%async_computation | async-start | bytes 524288 | tf_op jit(solution)/shard_map/all_to_all | solution.py:314
  17.4 1.3 %collective-permute-start.1 = (bf16[2,128,1024]{2,1,0:T(8,128)(2,1)}, bf16[2,128,1024]{2,1,0:T(8,128)(2,1)S(1)}, u32[]{:S(2)}, u32[]{:S(2)}) collective-permute-start(bf16[2,128,1024]{2,1,0:T(8,128)(2,1)} %get-tuple-element.40.kv_ref), channel_id=1, source_target_pairs={{0,2},{1,3},{4,6},{5,7},{8,10},{9,11},{12,14},{13,15},{16,18},{17,... | collective-permute-start | bytes 1572872 | tf_op jit(solution)/shard_map/ppermute | solution.py:312
  18.7 11.3 %all-to-all-done.mine_ref = bf16[32,16,256]{2,1,0:T(8,128)(2,1)S(1)} async-done(((bf16[32,16,256]{2,1,0:T(8,128)(2,1)}), bf16[32,16,256]{2,1,0:T(8,128)(2,1)S(1)}, u32[]{:S(2)}, u32[]{:S(2)}) %all-to-all-start) | async-done | bytes 262176 | tf_op jit(solution)/shard_map/all_to_all | solution.py:314
  29.9 0.0 collective-permute-start.2
  29.9 4.1 %collective-permute-done.1.far_ref = bf16[2,128,1024]{2,1,0:T(8,128)(2,1)S(1)} collective-permute-done((bf16[2,128,1024]{2,1,0:T(8,128)(2,1)}, bf16[2,128,1024]{2,1,0:T(8,128)(2,1)S(1)}, u32[]{:S(2)}, u32[]{:S(2)}) %collective-permute-start.1) | collective-permute-done | bytes 524320 | tf_op jit(solution)/shard_map/ppermute | solution.py:312
  34.1 0.0 collective-permute-done.2.other_ref
  34.1 0.7 copy-done.2
  34.7 0.6 shard_map.120.pr_ref
  35.3 0.1 collective-permute-start.4
  35.4 0.1 collective-permute-start.6
  35.5 2.2 %collective-permute-start.3 = (bf16[2,2,128,256]{3,2,1,0:T(8,128)(2,1)S(1)}, bf16[2,2,128,256]{3,2,1,0:T(8,128)(2,1)S(1)}, u32[]{:S(2)}, u32[]{:S(2)}) collective-permute-start(bf16[2,2,128,256]{3,2,1,0:T(8,128)(2,1)S(1)} %shard_map.120.pr_ref), channel_id=1, source_target_pairs={{0,3},{1,0},{2,1},{3,2},{4,7},{5,4},{6,5},{7,6},{8,11},{9,8},{10,9... | collective-permute-start | bytes 786440 | tf_op jit(solution)/shard_map/ppermute | solution.py:303
  37.7 3.9 %shard_map.121 = (bf16[128,8192]{1,0:T(8,128)(2,1)}, f32[2,128,1024]{2,1,0:T(8,128)S(1)}, bf16[2,128,1024]{2,1,0:T(8,128)(2,1)S(1)}, bf16[2,128,1024]{2,1,0:T(8,128)(2,1)}, bf16[2,2,128,256]{3,2,1,0:T(8,128)(2,1)S(1)}) custom-call(s32[1]{0:T(128)} %bitcast.sc_ref, s32[1,512]{1,0:T(1,128)S(1)} %copy-done.1, bf16[128,8192]{1,0:T(8,128)(2,1)} %q_ref.9, ...), custom_call_target="tpu_custom_call" | custom-call | flops 2684354560 | bytes 4194304 | tf_op jit(solution)/shard_map/pallas_call | solution.py:188
  41.6 6.0 %collective-permute-done.4.pr_ref = bf16[2,2,128,256]{3,2,1,0:T(8,128)(2,1)} collective-permute-done((bf16[2,2,128,256]{3,2,1,0:T(8,128)(2,1)S(1)}, bf16[2,2,128,256]{3,2,1,0:T(8,128)(2,1)}, u32[]{:S(2)}, u32[]{:S(2)}) %collective-permute-start.4) | collective-permute-done | bytes 262176 | tf_op jit(solution)/shard_map/ppermute | solution.py:303
  47.7 6.6 %shard_map.122 = (bf16[128,8192]{1,0:T(8,128)(2,1)}, f32[2,128,1024]{2,1,0:T(8,128)S(1)}, bf16[2,128,1024]{2,1,0:T(8,128)(2,1)S(1)}, bf16[2,128,1024]{2,1,0:T(8,128)(2,1)}, bf16[2,2,128,256]{3,2,1,0:T(8,128)(2,1)S(1)}) custom-call(s32[1]{0:T(128)} %bitcast.sc_ref, ...), custom_call_target="tpu_custom_call", output_to_operand_aliasing={{0}: (8, {}), {1}: (9, {}), {2}: (10, {}), {3}: (11, {})} | custom-call | flops 2684354560 | bytes 4194304 | tf_op jit(solution)/shard_map/pallas_call | solution.py:188
  54.3 6.7 %shard_map.123 = (bf16[128,8192]{1,0:T(8,128)(2,1)}, f32[2,128,1024]{2,1,0:T(8,128)S(1)}, bf16[2,128,1024]{2,1,0:T(8,128)(2,1)S(1)}, bf16[2,128,1024]{2,1,0:T(8,128)(2,1)}, bf16[2,2,128,256]{3,2,1,0:T(8,128)(2,1)S(1)}) custom-call(s32[1]{0:T(128)} %bitcast.sc_ref, ...), custom_call_target="tpu_custom_call", output_to_operand_aliasing={{0}: (8, {}), {1}: (9, {}), {2}: (10, {}), {3}: (11, {})} | custom-call | flops 2684354560 | bytes 4194304 | tf_op jit(solution)/shard_map/pallas_call | solution.py:188
  61.0 0.0 collective-permute-start.8
  61.0 1.1 %collective-permute-done.5.b_ref = bf16[2,2,128,256]{3,2,1,0:T(8,128)(2,1)S(1)} collective-permute-done((bf16[2,2,128,256]{3,2,1,0:T(8,128)(2,1)S(1)}, bf16[2,2,128,256]{3,2,1,0:T(8,128)(2,1)S(1)}, u32[]{:S(2)}, u32[]{:S(2)}) %collective-permute-start.5) | collective-permute-done | bytes 262176 | tf_op jit(solution)/shard_map/ppermute | solution.py:303
  62.1 6.6 %shard_map.124 = (bf16[128,8192]{1,0:T(8,128)(2,1)}, f32[2,128,1024]{2,1,0:T(8,128)S(1)}, bf16[2,128,1024]{2,1,0:T(8,128)(2,1)S(1)}, bf16[2,128,1024]{2,1,0:T(8,128)(2,1)}, bf16[2,2,128,256]{3,2,1,0:T(8,128)(2,1)S(1)}) custom-call(s32[1]{0:T(128)} %bitcast.sc_ref, ...), custom_call_target="tpu_custom_call", output_to_operand_aliasing={{0}: (8, {}), {1}: (9, {}), {2}: (10, {}), {3}: (11, {})} | custom-call | flops 2684354560 | bytes 4194304 | tf_op jit(solution)/shard_map/pallas_call | solution.py:188
  68.7 0.9 collective-permute-start.9
  69.6 4.0 %shard_map.125 = (bf16[128,8192]{1,0:T(8,128)(2,1)}, f32[2,128,1024]{2,1,0:T(8,128)S(1)}, bf16[2,128,1024]{2,1,0:T(8,128)(2,1)S(1)}, bf16[2,128,1024]{2,1,0:T(8,128)(2,1)}, bf16[2,2,128,256]{3,2,1,0:T(8,128)(2,1)S(1)}) custom-call(s32[1]{0:T(128)} %bitcast.sc_ref, ...), custom_call_target="tpu_custom_call", output_to_operand_aliasing={{0}: (8, {}), {1}: (9, {}), {2}: (10, {}), {3}: (11, {}), {... | custom-call | flops 2684354560 | bytes 4194304 | tf_op jit(solution)/shard_map/pallas_call | solution.py:188
  73.6 3.3 %collective-permute-start.7 = (bf16[2,128,1024]{2,1,0:T(8,128)(2,1)S(1)}, bf16[2,128,1024]{2,1,0:T(8,128)(2,1)S(1)}, u32[]{:S(2)}, u32[]{:S(2)}) collective-permute-start(bf16[2,128,1024]{2,1,0:T(8,128)(2,1)S(1)} %get-tuple-element.65), channel_id=1, source_target_pairs={{1,0},{2,1},{3,2},{5,4},{6,5},{7,6},{9,8},{10,9},{11,10},{13,12},{... | collective-permute-start | bytes 1572872 | tf_op jit(solution)/shard_map/ppermute | solution.py:332
  76.9 0.8 shard_map.126
  77.8 10.1 %collective-permute-start.10 = (bf16[2,128,1024]{2,1,0:T(8,128)(2,1)}, bf16[2,128,1024]{2,1,0:T(8,128)(2,1)}, u32[]{:S(2)}, u32[]{:S(2)}) collective-permute-start(bf16[2,128,1024]{2,1,0:T(8,128)(2,1)} %get-tuple-element.72), channel_id=1, source_target_pairs={{2,0},{3,1},{6,4},{7,5},{10,8},{11,9},{14,12},{15,13},{18,16},{19,... | collective-permute-start | bytes 1572872 | tf_op jit(solution)/shard_map/ppermute | solution.py:336
  87.9 1.5 %collective-permute-done.11 = bf16[32,16,256]{2,1,0:T(8,128)(2,1)S(1)} collective-permute-done((bf16[32,16,256]{2,1,0:T(8,128)(2,1)S(1)}, bf16[32,16,256]{2,1,0:T(8,128)(2,1)S(1)}, u32[]{:S(2)}, u32[]{:S(2)}) %collective-permute-start.11) | collective-permute-done | bytes 262176 | tf_op jit(solution)/shard_map/ppermute | solution.py:337
  89.4 0.8 add_convert_fusion.1
  90.2 9.2 %all-to-all-start.1 = ((bf16[32,16,256]{2,1,0:T(8,128)(2,1)}), bf16[32,16,256]{2,1,0:T(8,128)(2,1)S(1)}, u32[]{:S(2)}, u32[]{:S(2)}) async-start(bf16[32,16,256]{2,1,0:T(8,128)(2,1)} %add_convert_fusion.1), calls=%async_computation.1 | async-start | bytes 524288 | tf_op jit(solution)/shard_map/all_to_all | solution.py:339
  99.5 1.3 %add_convert_fusion = bf16[2,128,1024]{2,1,0:T(8,128)(2,1)S(1)} fusion(f32[2,128,1024]{2,1,0:T(8,128)S(1)} %get-tuple-element.64, bf16[2,128,1024]{2,1,0:T(8,128)(2,1)} %collective-permute-done.10, bf16[2,128,1024]{2,1,0:T(8,128)(2,1)S(1)} %collective-permute-done.7), kind=kLoop, calls=%fused_computation | loop fusion | flops 1310720 | bytes 2621440 | tf_op jit(solution)/shard_map/convert_element_type | solution.py:342
  100.8 0.8 slice_bitcast_fusion
  101.6 11.1 %all-to-all-done.1 = bf16[32,16,256]{2,1,0:T(8,128)(2,1)S(1)} async-done(((bf16[32,16,256]{2,1,0:T(8,128)(2,1)}), bf16[32,16,256]{2,1,0:T(8,128)(2,1)S(1)}, u32[]{:S(2)}, u32[]{:S(2)}) %all-to-all-start.1) | async-done | bytes 262176 | tf_op jit(solution)/shard_map/all_to_all | solution.py:339
  112.7 0.6 fusion
  (17 shorter events, 0.1 us)
Async XLA Ops:
  0.6 37.1 %copy-start.1 = (s32[1,512]{1,0:T(1,128)S(1)}, s32[1,512]{1,0:T(1,128)}, u32[]{:S(2)}) copy-start(s32[1,512]{1,0:T(1,128)} %seg_ref.9) | copy-start | bytes 6148
  2.6 35.1 %copy-start = (bf16[2,128,1024]{2,1,0:T(8,128)(2,1)S(1)}, bf16[2,128,1024]{2,1,0:T(8,128)(2,1)}, u32[]{:S(2)}) copy-start(bf16[2,128,1024]{2,1,0:T(8,128)(2,1)} %get-tuple-element.40.kv_ref) | copy-start | bytes 1572868
  2.6 27.3 %collective-permute-start = (bf16[2,128,1024]{2,1,0:T(8,128)(2,1)}, bf16[2,128,1024]{2,1,0:T(8,128)(2,1)S(1)}, u32[]{:S(2)}, u32[]{:S(2)}) collective-permute-start(bf16[2,128,1024]{2,1,0:T(8,128)(2,1)} %get-tuple-element.40.kv_ref), channel_id=1, source_target_pairs={{0,1},{1,2},{2,3},{4,5},{5,6},{6,7},{8,9},{9,10},{10,11},{12,13},{... | collective-permute-start | bytes 1572872 | tf_op jit(solution)/shard_map/ppermute | solution.py:311
  5.9 24.1 %all-to-all-start = ((bf16[32,16,256]{2,1,0:T(8,128)(2,1)}), bf16[32,16,256]{2,1,0:T(8,128)(2,1)S(1)}, u32[]{:S(2)}, u32[]{:S(2)}) async-start(bf16[32,16,256]{2,1,0:T(8,128)(2,1)} %get-tuple-element.41), calls=%async_computation | async-start | bytes 524288 | tf_op jit(solution)/shard_map/all_to_all | solution.py:314
  17.4 16.7 %collective-permute-start.1 = (bf16[2,128,1024]{2,1,0:T(8,128)(2,1)}, bf16[2,128,1024]{2,1,0:T(8,128)(2,1)S(1)}, u32[]{:S(2)}, u32[]{:S(2)}) collective-permute-start(bf16[2,128,1024]{2,1,0:T(8,128)(2,1)} %get-tuple-element.40.kv_ref), channel_id=1, source_target_pairs={{0,2},{1,3},{4,6},{5,7},{8,10},{9,11},{12,14},{13,15},{16,18},{17,... | collective-permute-start | bytes 1572872 | tf_op jit(solution)/shard_map/ppermute | solution.py:312
  29.9 4.1 %collective-permute-start.2 = (bf16[32,16,256]{2,1,0:T(8,128)(2,1)S(1)}, bf16[32,16,256]{2,1,0:T(8,128)(2,1)S(1)}, u32[]{:S(2)}, u32[]{:S(2)}) collective-permute-start(bf16[32,16,256]{2,1,0:T(8,128)(2,1)S(1)} %all-to-all-done.mine_ref), channel_id=1, source_target_pairs={{0,4},{4,0},{1,5},{5,1},{2,6},{6,2},{3,7},{7,3},{8,12},{12,8},{9,1... | collective-permute-start | bytes 786440 | tf_op jit(solution)/shard_map/ppermute | solution.py:316
  34.1 0.7 copy-start.2
  35.3 12.4 %collective-permute-start.4 = (bf16[2,2,128,256]{3,2,1,0:T(8,128)(2,1)S(1)}, bf16[2,2,128,256]{3,2,1,0:T(8,128)(2,1)}, u32[]{:S(2)}, u32[]{:S(2)}) collective-permute-start(bf16[2,2,128,256]{3,2,1,0:T(8,128)(2,1)S(1)} %shard_map.120.pr_ref), channel_id=1, source_target_pairs={{0,1},{1,2},{2,3},{3,0},{4,5},{5,6},{6,7},{7,4},{8,9},{9,10},{10,1... | collective-permute-start | bytes 786440 | tf_op jit(solution)/shard_map/ppermute | solution.py:303
  35.4 18.9 %collective-permute-start.6 = (bf16[2,2,128,256]{3,2,1,0:T(8,128)(2,1)S(1)}, bf16[2,2,128,256]{3,2,1,0:T(8,128)(2,1)S(1)}, u32[]{:S(2)}, u32[]{:S(2)}) collective-permute-start(bf16[2,2,128,256]{3,2,1,0:T(8,128)(2,1)S(1)} %shard_map.120.pr_ref), channel_id=1, source_target_pairs={{0,2},{1,3},{2,0},{3,1},{4,6},{5,7},{6,4},{7,5},{8,10},{9,11},{10,... | collective-permute-start | bytes 786440 | tf_op jit(solution)/shard_map/ppermute | solution.py:303
  35.5 25.5 %collective-permute-start.3 = (bf16[2,2,128,256]{3,2,1,0:T(8,128)(2,1)S(1)}, bf16[2,2,128,256]{3,2,1,0:T(8,128)(2,1)S(1)}, u32[]{:S(2)}, u32[]{:S(2)}) collective-permute-start(bf16[2,2,128,256]{3,2,1,0:T(8,128)(2,1)S(1)} %shard_map.120.pr_ref), channel_id=1, source_target_pairs={{0,3},{1,0},{2,1},{3,2},{4,7},{5,4},{6,5},{7,6},{8,11},{9,8},{10,9... | collective-permute-start | bytes 786440 | tf_op jit(solution)/shard_map/ppermute | solution.py:303
  54.3 7.8 %collective-permute-start.5 = (bf16[2,2,128,256]{3,2,1,0:T(8,128)(2,1)S(1)}, bf16[2,2,128,256]{3,2,1,0:T(8,128)(2,1)S(1)}, u32[]{:S(2)}, u32[]{:S(2)}) collective-permute-start(bf16[2,2,128,256]{3,2,1,0:T(8,128)(2,1)S(1)} %get-tuple-element.48), channel_id=1, source_target_pairs={{0,3},{1,0},{2,1},{3,2},{4,7},{5,4},{6,5},{7,6},{8,11},{9,8},{10,9... | collective-permute-start | bytes 786440 | tf_op jit(solution)/shard_map/ppermute | solution.py:303
  61.0 15.9 %collective-permute-start.8 = (bf16[2,2,128,256]{3,2,1,0:T(8,128)(2,1)S(1)}, bf16[2,2,128,256]{3,2,1,0:T(8,128)(2,1)S(1)}, u32[]{:S(2)}, u32[]{:S(2)}) collective-permute-start(bf16[2,2,128,256]{3,2,1,0:T(8,128)(2,1)S(1)} %get-tuple-element.68), channel_id=1, source_target_pairs={{0,2},{1,3},{2,0},{3,1},{4,6},{5,7},{6,4},{7,5},{8,10},{9,11},{10,... | collective-permute-start | bytes 786440 | tf_op jit(solution)/shard_map/ppermute | solution.py:303
  68.7 8.2 %collective-permute-start.9 = (bf16[2,2,128,256]{3,2,1,0:T(8,128)(2,1)S(1)}, bf16[2,2,128,256]{3,2,1,0:T(8,128)(2,1)S(1)}, u32[]{:S(2)}, u32[]{:S(2)}) collective-permute-start(bf16[2,2,128,256]{3,2,1,0:T(8,128)(2,1)S(1)} %get-tuple-element.69), channel_id=1, source_target_pairs={{0,1},{1,2},{2,3},{3,0},{4,5},{5,6},{6,7},{7,4},{8,9},{9,10},{10,1... | collective-permute-start | bytes 786440 | tf_op jit(solution)/shard_map/ppermute | solution.py:303
  69.6 7.3 %copy-start.3 = (s32[1,2]{1,0:T(1,128)S(1)}, s32[1,2]{1,0:T(1,128)}, u32[]{:S(2)}) copy-start(s32[1,2]{1,0:T(1,128)} %group_ref.3) | copy-start | bytes 28
  73.6 25.9 %collective-permute-start.7 = (bf16[2,128,1024]{2,1,0:T(8,128)(2,1)S(1)}, bf16[2,128,1024]{2,1,0:T(8,128)(2,1)S(1)}, u32[]{:S(2)}, u32[]{:S(2)}) collective-permute-start(bf16[2,128,1024]{2,1,0:T(8,128)(2,1)S(1)} %get-tuple-element.65), channel_id=1, source_target_pairs={{1,0},{2,1},{3,2},{5,4},{6,5},{7,6},{9,8},{10,9},{11,10},{13,12},{... | collective-permute-start | bytes 1572872 | tf_op jit(solution)/shard_map/ppermute | solution.py:332
  77.8 21.7 %collective-permute-start.10 = (bf16[2,128,1024]{2,1,0:T(8,128)(2,1)}, bf16[2,128,1024]{2,1,0:T(8,128)(2,1)}, u32[]{:S(2)}, u32[]{:S(2)}) collective-permute-start(bf16[2,128,1024]{2,1,0:T(8,128)(2,1)} %get-tuple-element.72), channel_id=1, source_target_pairs={{2,0},{3,1},{6,4},{7,5},{10,8},{11,9},{14,12},{15,13},{18,16},{19,... | collective-permute-start | bytes 1572872 | tf_op jit(solution)/shard_map/ppermute | solution.py:336
  87.9 1.5 %collective-permute-start.11 = (bf16[32,16,256]{2,1,0:T(8,128)(2,1)S(1)}, bf16[32,16,256]{2,1,0:T(8,128)(2,1)S(1)}, u32[]{:S(2)}, u32[]{:S(2)}) collective-permute-start(bf16[32,16,256]{2,1,0:T(8,128)(2,1)S(1)} %get-tuple-element.74), channel_id=1, source_target_pairs={{0,4},{4,0},{1,5},{5,1},{2,6},{6,2},{3,7},{7,3},{8,12},{12,8},{9,1... | collective-permute-start | bytes 786440 | tf_op jit(solution)/shard_map/ppermute | solution.py:337
  90.2 22.5 %all-to-all-start.1 = ((bf16[32,16,256]{2,1,0:T(8,128)(2,1)}), bf16[32,16,256]{2,1,0:T(8,128)(2,1)S(1)}, u32[]{:S(2)}, u32[]{:S(2)}) async-start(bf16[32,16,256]{2,1,0:T(8,128)(2,1)} %add_convert_fusion.1), calls=%async_computation.1 | async-start | bytes 524288 | tf_op jit(solution)/shard_map/all_to_all | solution.py:339
